TPU v7x, 32 devices: a whole 2x2x4 slice. The times are simulated.
32 devices in a mesh: section: 2 (over core), wide: 8 (over z, x), fc: 2 (over y).
Axes of the slice: x: 2, y: 2, z: 4, core: 2. Of those that a mesh axis runs over, the one named last changes fastest.
Arguments:
- map_p2: float32 [8, 48, 96, 256], P('wide', 'section', None, 'fc'), may hold values from -6 to 6
- map_p3: float32 [8, 24, 48, 256], P('wide', 'section', None, 'fc'), may hold values from -6 to 6
- map_p4: float32 [8, 12, 24, 256], P('wide', 'section', None, 'fc'), may hold values from -6 to 6
- map_p5: float32 [8, 6, 12, 256], P('wide', 'section', None, 'fc'), may hold values from -6 to 6
- boxes: float32 [4096, 4], P('wide'), may hold values from 0.2 to 0.8
- levels: int32 [4096], P('wide'), may hold values from 0 to 3
- classes: int32 [4096], P('wide'), may hold values from 0 to 80
- sampled: int32 [4096], P('wide'), may hold values 0 or 1
- counts: int32 [8], P('wide'), may hold values from 1 to 512, as said below
- targets: float32 [4096, 4], P('wide'), may hold values from -6 to 6
- first_weight: float32 [12544, 1024], P('fc', ('section', 'wide')), may hold values from -0.0546875 to 0.0546875
- second_weight: float32 [1024, 1024], P('fc', ('section', 'wide')), may hold values from -0.1875 to 0.1875
- out_weight: float32 [1024, 401], P(('section', 'wide', 'fc')), may hold values from -0.75 to 0.75
- hidden_bias: float32 [1024, 2], P(('section', 'wide', 'fc')), may hold values from -2 to 2
- out_bias: float32 [401], replicated, may hold values from -2 to 2
- first_moment: float32 [12544, 1024], P('fc', ('section', 'wide')), may hold values from -0.0034179688 to 0.0034179688
- second_moment: float32 [1024, 1024], P('fc', ('section', 'wide')), may hold values from -0.0068359375 to 0.0068359375
- out_moment: float32 [1024, 401], P(('section', 'wide', 'fc')), may hold values from -0.0625 to 0.0625
- hidden_moment: float32 [1024, 2], P(('section', 'wide', 'fc')), may hold values from -0.0234375 to 0.0234375
- bias_moment: float32 [401], replicated, may hold values from -0.3125 to 0.3125
- first_average: float32 [12544, 1024], P('fc', ('section', 'wide')), may hold values from -0.0546875 to 0.0546875
- second_average: float32 [1024, 1024], P('fc', ('section', 'wide')), may hold values from -0.1875 to 0.1875
- out_average: float32 [1024, 401], P(('section', 'wide', 'fc')), may hold values from -0.75 to 0.75
- hidden_average: float32 [1024, 2], P(('section', 'wide', 'fc')), may hold values from -2 to 2
- bias_average: float32 [401], replicated, may hold values from -2 to 2
Outputs:
- loss_sum: float32 [], replicated
- roi_count: float32 [], replicated
- grad_p2: float32 [8, 48, 96, 256], P('wide', 'section', None, 'fc')
- grad_p3: float32 [8, 24, 48, 256], P('wide', 'section', None, 'fc')
- grad_p4: float32 [8, 12, 24, 256], P('wide', 'section', None, 'fc')
- grad_p5: float32 [8, 6, 12, 256], P('wide', 'section', None, 'fc')
- first_new: float32 [12544, 1024], P('fc', ('section', 'wide'))
- first_moment_new: float32 [12544, 1024], P('fc', ('section', 'wide'))
- first_average_new: float32 [12544, 1024], P('fc', ('section', 'wide'))
- second_new: float32 [1024, 1024], P('fc', ('section', 'wide'))
- second_moment_new: float32 [1024, 1024], P('fc', ('section', 'wide'))
- second_average_new: float32 [1024, 1024], P('fc', ('section', 'wide'))
- out_new: float32 [1024, 401], P(('section', 'wide', 'fc'))
- out_moment_new: float32 [1024, 401], P(('section', 'wide', 'fc'))
- out_average_new: float32 [1024, 401], P(('section', 'wide', 'fc'))
- hidden_new: float32 [1024, 2], P(('section', 'wide', 'fc'))
- hidden_moment_new: float32 [1024, 2], P(('section', 'wide', 'fc'))
- hidden_average_new: float32 [1024, 2], P(('section', 'wide', 'fc'))
- bias_new: float32 [401], replicated
- bias_moment_new: float32 [401], replicated
- bias_average_new: float32 [401], replicated
Inputs may be any that keep to these rules, and one draw needn't show every extreme that they name: The live slots of each image are its first counts slots; one image uses all 512.
All inputs are finite; a program needn't handle non-finite values. No bound on the sum of `sampled` on one device may be relied on, other than what follows from the above.
Results may differ from a plain program's by a relative error of at most 0.02.
Values may be sent and summed in bfloat16 or wider, within the bound.
No kernel may reach another device: no remote copies, remote signals or barrier semaphores. Data moves between devices by JAX's collectives and lax.ppermute only.
A program may use at most 640 MiB of HBM per device.

v0:
```python
import math

import jax
import jax.numpy as jnp
from jax import lax
from jax.sharding import PartitionSpec as P

CLASSES = 81
MICRO = 4


MOMENTUM = 0.9
AVERAGE = 0.7
DECAY = 0.0001
SMOOTH = 0.5


def from_behind(value, axis, steps):
    count = lax.axis_size(axis)
    first, last = (max(0, -steps), min(count, count - steps))
    return lax.ppermute(value, axis, [(source, source + steps) for source in range(first, last)])


def sample_cells(boxes, level, height, width, parts):
    shapes = [(height >> depth, width >> depth) for depth in range(4)]
    held = [rows // parts for rows, cols in shapes]
    starts = [0]
    for depth in range(3):
        starts.append(starts[-1] + held[depth] * shapes[depth][1])
    half_total = starts[3] + held[3] * shapes[3][1]
    matches = level[:, None] == jnp.arange(4, dtype=jnp.int32)[None, :]

    def choose(values):
        table = jnp.asarray(values, dtype=jnp.int32)[None, :]
        return jnp.sum(jnp.where(matches, table, 0), axis=1)

    level_rows = choose([rows for rows, cols in shapes])
    level_cols = choose([cols for rows, cols in shapes])
    level_held = choose(held)
    level_start = choose(starts)
    fraction = (
        jnp.arange(7, dtype=jnp.float32)[:, None]
        + (jnp.arange(2, dtype=jnp.float32)[None, :] + 0.5) * 0.5
    ) / 7.0

    def corners(center, extent, count):
        reach = (count - 1).astype(jnp.float32)
        anchor = (center - 0.25 * extent) * reach
        length = 0.5 * extent * reach
        points = anchor[:, None, None] + length[:, None, None] * fraction[None]
        lower = jnp.clip(jnp.floor(points), 0.0, (count - 2).astype(jnp.float32)[:, None, None])
        upper_weight = points - lower
        index = lower.astype(jnp.int32)[..., None] + jnp.arange(2, dtype=jnp.int32)
        weight = jnp.stack([1.0 - upper_weight, upper_weight], axis=-1)
        return (index, weight)

    row_index, row_weight = corners(boxes[:, 0], boxes[:, 2], level_rows)
    col_index, col_weight = corners(boxes[:, 1], boxes[:, 3], level_cols)
    held_b = level_held[:, None, None, None]
    owner = row_index // held_b
    local_row = row_index - owner * held_b
    row_cells = (
        owner * half_total
        + level_start[:, None, None, None]
        + local_row * level_cols[:, None, None, None]
    )
    cells = row_cells[:, :, :, :, None, None, None] + col_index[:, None, None, None, :, :, :]
    weights = (
        0.25 * row_weight[:, :, :, :, None, None, None] * col_weight[:, None, None, None, :, :, :]
    )
    return (cells, weights)


def crop_rows(table, cells, weights):
    values = table[cells]
    summed = jnp.einsum("rijakmbc,rijakmb->rcik", values, weights, precision=lax.Precision.HIGHEST)
    return summed.reshape(summed.shape[0], -1)


def row_losses(logits, classes, live, targets):
    scores = logits[:, :CLASSES]
    deltas = logits[:, CLASSES:].reshape(logits.shape[0], CLASSES - 1, 4)
    matches = classes[:, None] == jnp.arange(CLASSES, dtype=jnp.int32)[None, :]
    entropy = jax.nn.logsumexp(scores, axis=1) - jnp.sum(jnp.where(matches, scores, 0.0), axis=1)
    chosen_class = classes[:, None] == jnp.arange(1, CLASSES, dtype=jnp.int32)[None, :]
    chosen = jnp.sum(jnp.where(chosen_class[:, :, None], deltas, 0.0), axis=1)
    offset = chosen - targets
    magnitude = jnp.abs(offset)
    smooth = jnp.where(magnitude < SMOOTH, 0.5 * offset * offset / SMOOTH, magnitude - 0.5 * SMOOTH)
    foreground = (classes > 0).astype(logits.dtype)
    return live * (entropy + foreground * jnp.sum(smooth, axis=1))


def renew(weight, moment, average, grad, rate):
    step_value = grad + DECAY * weight
    moment_new = MOMENTUM * moment + step_value
    weight_new = weight - rate * (step_value + MOMENTUM * moment_new)
    average_new = AVERAGE * average + (1.0 - AVERAGE) * weight_new
    return (weight_new, moment_new, average_new)


def contract_rows(left, right):
    return lax.dot_general(
        left, right, (((0,), (0,)), ((), ())), preferred_element_type=jnp.float32
    )


def contract_cols(left, right):
    return lax.dot_general(
        left, right, (((1,), (1,)), ((), ())), preferred_element_type=jnp.float32
    )


def product(left, right):
    return jnp.dot(left, right, preferred_element_type=jnp.float32)


def only_where(flag, work, *operands):

    def skipped(*values):
        return jax.tree.map(jnp.zeros_like, work(*values))

    return lax.cond(flag, work, skipped, *operands)


def body(
    map_p2,
    map_p3,
    map_p4,
    map_p5,
    boxes,
    levels,
    classes,
    sampled,
    counts,
    targets,
    first_weight,
    second_weight,
    out_weight,
    hidden_bias,
    out_bias,
    first_moment,
    second_moment,
    out_moment,
    hidden_moment,
    bias_moment,
    first_average,
    second_average,
    out_average,
    hidden_average,
    bias_average,
):
    n_section = lax.axis_size("section")
    n_fc = lax.axis_size("fc")
    n_wide = lax.axis_size("wide")
    section_pos = lax.axis_index("section")
    fc_pos = lax.axis_index("fc")
    crop_flag = section_pos == 0
    head_flag = section_pos == 1
    head_value = head_flag.astype(jnp.float32)
    maps = [map_p2, map_p3, map_p4, map_p5]
    channels = map_p2.shape[3]
    height = map_p2.shape[1] * n_section
    width = map_p2.shape[2]
    half_table = jnp.concatenate([level_map[0].reshape(-1, channels) for level_map in maps], axis=0)
    table = lax.all_gather(half_table, "section", axis=0, tiled=True)
    rows_dev = boxes.shape[0]
    rows_micro = rows_dev // MICRO
    rows_head = rows_micro // n_fc
    w_first, w_second = (
        lax.all_gather(first_weight.astype(jnp.bfloat16), ("section", "wide"), axis=1, tiled=True),
        lax.all_gather(second_weight.astype(jnp.bfloat16), ("section", "wide"), axis=1, tiled=True),
    )
    w_out, b_hidden = (
        lax.all_gather(
            out_weight.astype(jnp.bfloat16), ("section", "wide", "fc"), axis=0, tiled=True
        ),
        lax.all_gather(
            hidden_bias.astype(jnp.bfloat16), ("section", "wide", "fc"), axis=0, tiled=True
        ),
    )
    hidden = w_first.shape[1]
    hidden_part = hidden // n_fc
    bias_first = lax.dynamic_slice_in_dim(b_hidden[:, 0], fc_pos * hidden_part, hidden_part).astype(
        jnp.float32
    )
    bias_second = b_hidden[:, 1].astype(jnp.float32)
    live = ((jnp.arange(rows_dev, dtype=jnp.int32) < counts[0]) & (sampled > 0)).astype(jnp.float32)
    total = lax.psum(jnp.sum(live), "wide")
    scale = head_value / total

    def micro_cells(index):
        start = index * rows_micro
        return sample_cells(
            boxes[start : start + rows_micro],
            levels[start : start + rows_micro],
            height,
            width,
            n_section,
        )

    def crop_forward(index):
        cells, weights = micro_cells(index)
        crops = only_where(crop_flag, crop_rows, table, cells, weights)
        return crops.astype(jnp.bfloat16)

    def crop_backward(index, grad_inputs):
        cells, weights = micro_cells(index)

        def spread(values_table, grad_values):
            return jax.vjp(lambda entries: crop_rows(entries, cells, weights), values_table)[1](
                grad_values.astype(jnp.float32)
            )[0]

        return only_where(crop_flag, spread, table, grad_inputs)

    def head_step(index, inputs):
        first_row = index * rows_micro
        partial_value = only_where(head_flag, product, inputs, w_first)
        pre_first = (
            lax.psum_scatter(partial_value, "fc", scatter_dimension=1, tiled=True) + bias_first
        )
        act_first, back_first = jax.vjp(jax.nn.gelu, pre_first)
        act_first = act_first.astype(jnp.bfloat16)
        pre_second = (
            lax.psum_scatter(
                product(act_first, w_second).astype(jnp.bfloat16),
                "fc",
                scatter_dimension=0,
                tiled=True,
            ).astype(jnp.float32)
            + bias_second
        )
        act_second, back_second = jax.vjp(jax.nn.gelu, pre_second)
        act_second = act_second.astype(jnp.bfloat16)
        logits = product(act_second, w_out) + out_bias
        own_start = first_row + fc_pos * rows_head
        own_classes = lax.dynamic_slice_in_dim(classes, own_start, rows_head)
        own_live = lax.dynamic_slice_in_dim(live, own_start, rows_head)
        own_targets = lax.dynamic_slice_in_dim(targets, own_start, rows_head, 0)
        loss_part, back_loss = jax.vjp(
            lambda values: jnp.sum(row_losses(values, own_classes, own_live, own_targets)), logits
        )
        grad_logits = back_loss(scale)[0].astype(jnp.bfloat16)
        grad_second = back_second(contract_cols(grad_logits, w_out))[0].astype(jnp.bfloat16)
        grad_second_all = lax.all_gather(grad_second, "fc", axis=0, tiled=True)
        grad_first = back_first(contract_cols(grad_second_all, w_second))[0].astype(jnp.bfloat16)
        grad_first_all = lax.all_gather(grad_first, "fc", axis=1, tiled=True)
        grad_inputs = only_where(head_flag, contract_cols, grad_first_all, w_first).astype(
            jnp.bfloat16
        )
        first_term = only_where(head_flag, contract_rows, inputs, grad_first_all)
        first_bias_grad = lax.dynamic_update_slice(
            jnp.zeros((hidden,), jnp.float32),
            jnp.sum(grad_first.astype(jnp.float32), axis=0),
            (fc_pos * hidden_part,),
        )
        bias_terms = jnp.stack(
            [first_bias_grad, jnp.sum(grad_second.astype(jnp.float32), axis=0)], axis=1
        )
        terms = (
            first_term,
            contract_rows(act_first, grad_second_all),
            contract_rows(act_second, grad_logits),
            bias_terms,
        )
        return (
            loss_part * head_value,
            jnp.sum(grad_logits.astype(jnp.float32), axis=0),
            grad_inputs,
            terms,
        )

    table_grad = jnp.zeros_like(table)
    loss_local = jnp.zeros((), jnp.float32)
    bias_out_grad = jnp.zeros(out_bias.shape, jnp.float32)
    totals = None
    inbox = None
    behind = None
    for tick in range(MICRO + 2):
        if behind is not None:
            table_grad = table_grad + crop_backward(tick - 2, behind)
        ahead = crop_forward(tick) if tick < MICRO else None
        grad_inputs = None
        if inbox is not None:
            loss_part, bias_part, grad_inputs, terms = head_step(tick - 1, inbox)
            loss_local = loss_local + loss_part
            bias_out_grad = bias_out_grad + bias_part
            if totals is None:
                totals = terms
            else:
                totals = tuple((before + after for before, after in zip(totals, terms)))
        inbox = from_behind(ahead, "section", 1) if ahead is not None else None
        behind = from_behind(grad_inputs, "section", -1) if grad_inputs is not None else None
    layer_sums = (
        lax.psum_scatter(totals[0], ("section", "wide"), scatter_dimension=1, tiled=True),
        lax.psum_scatter(totals[1], ("section", "wide"), scatter_dimension=1, tiled=True),
    )
    output_sums = (
        lax.psum_scatter(totals[2], ("section", "wide", "fc"), scatter_dimension=0, tiled=True),
        lax.psum_scatter(totals[3], ("section", "wide", "fc"), scatter_dimension=0, tiled=True),
    )
    loss_sum, bias_total = lax.psum((loss_local, bias_out_grad), ("section", "wide", "fc"))
    own_grad = lax.psum_scatter(
        table_grad.astype(jnp.bfloat16), "section", scatter_dimension=0, tiled=True
    ).astype(jnp.float32)
    map_grads = []
    start_cell = 0
    for level_map in maps:
        cell_count = level_map.shape[1] * level_map.shape[2]
        map_grads.append(own_grad[start_cell : start_cell + cell_count].reshape(level_map.shape))
        start_cell = start_cell + cell_count
    rate = 0.15 * math.sqrt(rows_dev * n_wide)
    first_out = renew(first_weight, first_moment, first_average, layer_sums[0], rate)
    second_out = renew(second_weight, second_moment, second_average, layer_sums[1], rate)
    out_out = renew(out_weight, out_moment, out_average, output_sums[0], rate)
    hidden_out = renew(hidden_bias, hidden_moment, hidden_average, output_sums[1], rate)
    bias_out = renew(out_bias, bias_moment, bias_average, bias_total, 4.0)
    return (
        loss_sum,
        total,
        map_grads[0],
        map_grads[1],
        map_grads[2],
        map_grads[3],
        first_out[0],
        first_out[1],
        first_out[2],
        second_out[0],
        second_out[1],
        second_out[2],
        out_out[0],
        out_out[1],
        out_out[2],
        hidden_out[0],
        hidden_out[1],
        hidden_out[2],
        bias_out[0],
        bias_out[1],
        bias_out[2],
    )


def solution(mesh):
    in_specs = (
        P("wide", "section", None, "fc"),
        P("wide", "section", None, "fc"),
        P("wide", "section", None, "fc"),
        P("wide", "section", None, "fc"),
        P("wide", None),
        P("wide"),
        P("wide"),
        P("wide"),
        P("wide"),
        P("wide", None),
        P("fc", ("section", "wide")),
        P("fc", ("section", "wide")),
        P(("section", "wide", "fc"), None),
        P(("section", "wide", "fc"), None),
        P(),
        P("fc", ("section", "wide")),
        P("fc", ("section", "wide")),
        P(("section", "wide", "fc"), None),
        P(("section", "wide", "fc"), None),
        P(),
        P("fc", ("section", "wide")),
        P("fc", ("section", "wide")),
        P(("section", "wide", "fc"), None),
        P(("section", "wide", "fc"), None),
        P(),
    )
    out_specs = (
        P(),
        P(),
        P("wide", "section", None, "fc"),
        P("wide", "section", None, "fc"),
        P("wide", "section", None, "fc"),
        P("wide", "section", None, "fc"),
        P("fc", ("section", "wide")),
        P("fc", ("section", "wide")),
        P("fc", ("section", "wide")),
        P("fc", ("section", "wide")),
        P("fc", ("section", "wide")),
        P("fc", ("section", "wide")),
        P(("section", "wide", "fc"), None),
        P(("section", "wide", "fc"), None),
        P(("section", "wide", "fc"), None),
        P(("section", "wide", "fc"), None),
        P(("section", "wide", "fc"), None),
        P(("section", "wide", "fc"), None),
        P(),
        P(),
        P(),
    )
    return jax.shard_map(body, mesh=mesh, in_specs=in_specs, out_specs=out_specs, check_vma=False)
```

profile of v0, /device:TPU:1, one launch (start us, length us, event | category | flops | bytes accessed | tf_op | source)
XLA Modules:
  0.0 5437.6 jit_solution(15722635813371859636)
XLA Ops:
  22.1 78.5 %iota_add_fusion.2 = (s32[128,7,2,2]{3,2,1,0:T(2,128)}, s32[128,7,2,2]{3,2,1,0:T(2,128)}, s32[128,7,2,2]{3,2,1,0:T(2,128)}, s32[128,7,2,2]{3,2,1,0:T(2,128)}) fusion(s32[128,7,2]{2,1,0:T(8,128)S(1)} %copy.569, s32[128]{0:T(128)} %get-tuple-element.1989, s32[128]{0:T(128)S(1)} %fusion.140, s32[128]{0:T(128)S(1)} %get-tuple-element.1994, s32[128]{0:T(128)S(1)} %fusion.141, ...), kind=kLoop, calls=%fused_computation.103 | loop fusion | flops 64512 | bytes 73728 | tf_op jit(solution)/shard_map/add | solution.py:53
  131.6 485.8 %collective-permute-done.1 = bf16[128,6272]{1,0:T(8,128)(2,1)} collective-permute-done((bf16[128,6272]{1,0:T(8,128)(2,1)}, bf16[128,6272]{1,0:T(8,128)(2,1)}, u32[]{:S(2)}, u32[]{:S(2)}) %collective-permute-start.1) | collective-permute-done | bytes 1605664 | tf_op jit(solution)/shard_map/ppermute | solution.py:21
  617.4 10.2 conditional.23
  617.4 10.2 fusion.174
  628.2 78.5 %iota_add_fusion = (s32[128,7,2,2]{3,2,1,0:T(2,128)}, s32[128,7,2,2]{3,2,1,0:T(2,128)}, s32[128,7,2,2]{3,2,1,0:T(2,128)}, s32[128,7,2,2]{3,2,1,0:T(2,128)}) fusion(s32[128,7,2]{2,1,0:T(8,128)} %copy.587, s32[128]{0:T(128)S(1)} %copy-done.83, s32[128]{0:T(128)S(1)} %copy-done.112, s32[128]{0:T(128)S(1)} %copy-done.86, s32[128]{0:T(128)S(1)} %copy-done.113, ...), kind=kLoop, calls=%fused_computation.101 | loop fusion | flops 64512 | bytes 73728 | tf_op jit(solution)/shard_map/add | solution.py:53
  716.4 415.4 %collective-permute-done = bf16[128,6272]{1,0:T(8,128)(2,1)} collective-permute-done((bf16[128,6272]{1,0:T(8,128)(2,1)}, bf16[128,6272]{1,0:T(8,128)(2,1)}, u32[]{:S(2)}, u32[]{:S(2)}) %collective-permute-start) | collective-permute-done | bytes 1605664 | tf_op jit(solution)/shard_map/ppermute | solution.py:21
  1131.7 10.2 conditional.21
  1131.7 10.2 fusion.173
  1151.0 569.0 %collective-permute-done.2 = bf16[128,6272]{1,0:T(8,128)(2,1)} collective-permute-done((bf16[128,6272]{1,0:T(8,128)(2,1)}, bf16[128,6272]{1,0:T(8,128)(2,1)}, u32[]{:S(2)}, u32[]{:S(2)}) %collective-permute-start.2) | collective-permute-done | bytes 1605664 | tf_op jit(solution)/shard_map/ppermute | solution.py:21
  1720.0 9.4 conditional.25
  1720.0 9.4 fusion.175
  1730.3 495.2 %collective-permute-done.3 = bf16[128,6272]{1,0:T(8,128)(2,1)S(1)} collective-permute-done((bf16[128,6272]{1,0:T(8,128)(2,1)}, bf16[128,6272]{1,0:T(8,128)(2,1)S(1)}, u32[]{:S(2)}, u32[]{:S(2)}) %collective-permute-start.3) | collective-permute-done | bytes 1605664 | tf_op jit(solution)/shard_map/ppermute | solution.py:21
  2225.5 8.9 conditional.27
  2225.5 8.9 fusion.176
  2235.9 66.0 %all-gather.1 = bf16[32,32,2]{1,2,0:T(2,128)(2,1)S(1)} all-gather(bf16[1,32,2]{1,2,0:T(2,128)(2,1)S(1)} %convert_bitcast_fusion), channel_id=1, replica_groups=mesh['section'=2,'wide'=8,'fc'=2] {'section','wide','fc'}, dimensions={0}, use_global_device_ids=true | all-gather | bytes 4224 | tf_op jit(solution)/shard_map/all_gather | solution.py:178
  2305.4 14.6 psum.22
  2324.0 81.3 %all_gather.43 = bf16[1024,401]{1,0:T(8,128)(2,1)} all-gather(bf16[32,401]{1,0:T(8,128)(2,1)S(1)} %convert_element_type.649), channel_id=1, replica_groups=mesh['section'=2,'wide'=8,'fc'=2] {'section','wide','fc'}, dimensions={0}, use_global_device_ids=true | all-gather | bytes 846912 | tf_op jit(solution)/shard_map/all_gather | solution.py:175
  2420.9 12.5 reduce-scatter.31.cloned.1.call-done
  2454.5 5.0 all_gather.48
  2463.7 4.5 all_gather.44
  2470.8 4.5 all_gather.50
  2477.9 4.5 all_gather.46
  2493.9 4.5 all_gather.47
  2498.4 5.7 all_gather.49
  2504.1 4.9 all_gather.51
  2509.1 5.0 all_gather.45
  2520.3 11.8 conditional.37
  2520.3 11.8 fusion.182
  2532.1 11.8 conditional.38
  2532.1 11.8 fusion.183
  2543.9 10.6 conditional.39
  2544.1 10.4 fusion.184
  2554.5 11.8 conditional.36
  2554.5 11.8 fusion.181
  2566.3 41.3 add_add_fusion
  2607.6 7.4 conditional.32
  2608.3 6.7 fusion.179
  2619.7 6.6 conditional.30
  2619.7 6.6 fusion.178
  2631.0 7.0 conditional.34
  2631.4 6.6 fusion.180
  2643.1 7.9 conditional.28
  2643.1 7.9 fusion.177
  2662.4 38.3 all-reduce.10
  2709.1 12.4 conditional.35
  2723.0 5.5 add_convert_fusion
  2728.5 2685.6 %fusion = bf16[3072,128]{1,0:T(8,128)(2,1)S(1)} fusion(bf16[6120,128]{1,0:T(8,128)(2,1)} %add_convert_fusion), kind=kCustom, calls=%all-reduce-scatter | all-reduce-scatter fusion | flops 786433 | bytes 2353664
  5425.1 5.6 multiply_add_fusion.8
  (459 shorter events, 190.8 us)
Async XLA Ops:
  7.2 95.9 %all-gather.10.cloned.1.call-start = ((), (), s32[]{:S(2)}) async-start(), calls=%async_computation.25 | async-start | bytes 4706304 | tf_op jit(solution)/shard_map/all_gather | solution.py:166
  10.7 606.7 %all-gather.6.cloned.1.call-start = ((), (), s32[]{:S(2)}) async-start(), calls=%async_computation.12 | async-start | bytes 13647872 | tf_op jit(solution)/shard_map/all_gather | solution.py:171
  13.2 2289.0 %all-gather.8.cloned.1.call-start = ((), (), s32[]{:S(2)}) async-start(), calls=%async_computation.14 | async-start | bytes 1114112 | tf_op jit(solution)/shard_map/all_gather | solution.py:172
  14.8 2287.4 %reduce-scatter.21.cloned.1.call-start = ((), (), s32[]{:S(2)}) async-start(), calls=%async_computation.16 | async-start | bytes 786432 | tf_op jit(solution)/shard_map/reduce_scatter | solution.py:221
  114.6 502.9 %collective-permute-start.1 = (bf16[128,6272]{1,0:T(8,128)(2,1)}, bf16[128,6272]{1,0:T(8,128)(2,1)}, u32[]{:S(2)}, u32[]{:S(2)}) collective-permute-start(bf16[128,6272]{1,0:T(8,128)(2,1)} %copy.575), channel_id=1, source_target_pairs={{0,16},{1,17},{2,18},{3,19},{4,20},{5,21},{6,22},{7,23},{8,24},{9,... | collective-permute-start | bytes 4816904 | tf_op jit(solution)/shard_map/ppermute | solution.py:21
  126.4 501.8 %copy-start.83 = (s32[128]{0:T(128)S(1)}, s32[128]{0:T(128)}, u32[]{:S(2)}) copy-start(s32[128]{0:T(128)} %get-tuple-element.1990) | copy-start | bytes 1540
  126.4 501.8 %copy-start.86 = (s32[128]{0:T(128)S(1)}, s32[128]{0:T(128)}, u32[]{:S(2)}) copy-start(s32[128]{0:T(128)} %get-tuple-element.1991) | copy-start | bytes 1540
  126.4 501.8 %copy-start.112 = (s32[128]{0:T(128)S(1)}, s32[128]{0:T(128)}, u32[]{:S(2)}) copy-start(s32[128]{0:T(128)} %fusion.138) | copy-start | bytes 1540
  126.5 580.3 %copy-start.64 = (f32[128,7,2,1,1,1,1]{0,2,6,5,4,3,1:T(2,128)S(1)}, f32[128,7,2,1,1,1,1]{0,2,6,5,4,3,1:T(2,128)}, u32[]{:S(2)}) copy-start(f32[128,7,2,1,1,1,1]{0,2,6,5,4,3,1:T(2,128)} %get-tuple-element.2038) | copy-start | bytes 21508
  126.5 580.3 %copy-start.65 = (f32[128,7,2,1,1,1,1]{0,2,6,5,4,3,1:T(2,128)S(1)}, f32[128,7,2,1,1,1,1]{0,2,6,5,4,3,1:T(2,128)}, u32[]{:S(2)}) copy-start(f32[128,7,2,1,1,1,1]{0,2,6,5,4,3,1:T(2,128)} %get-tuple-element.2039) | copy-start | bytes 21508
  126.5 580.9 %copy-start.66 = (f32[128,7,2,1]{0,3,2,1:T(1,128)S(1)}, f32[128,7,2,1]{0,3,2,1:T(1,128)}, u32[]{:S(2)}) copy-start(f32[128,7,2,1]{0,3,2,1:T(1,128)} %get-tuple-element.2036) | copy-start | bytes 21508
  126.5 580.9 %copy-start.67 = (f32[128,7,2,1]{0,3,2,1:T(1,128)S(1)}, f32[128,7,2,1]{0,3,2,1:T(1,128)}, u32[]{:S(2)}) copy-start(f32[128,7,2,1]{0,3,2,1:T(1,128)} %get-tuple-element.2037) | copy-start | bytes 21508
  126.5 581.5 %copy-start.92 = (s32[128]{0:T(128)S(1)}, s32[128]{0:T(128)}, u32[]{:S(2)}) copy-start(s32[128]{0:T(128)} %copy-done.91) | copy-start | bytes 1540
  126.5 581.5 %copy-start.94 = (s32[128]{0:T(128)S(1)}, s32[128]{0:T(128)}, u32[]{:S(2)}) copy-start(s32[128]{0:T(128)} %copy-done.93) | copy-start | bytes 1540
  126.5 583.2 %copy-start.52 = (s32[128,7,2,1]{0,3,2,1:T(1,128)S(1)}, s32[128,7,2,1]{0,3,2,1:T(1,128)}, u32[]{:S(2)}) copy-start(s32[128,7,2,1]{0,3,2,1:T(1,128)} %get-tuple-element.2092) | copy-start | bytes 21508
  126.5 583.2 %copy-start.79 = (s32[128]{0:T(128)S(1)}, s32[128]{0:T(128)}, u32[]{:S(2)}) copy-start(s32[128]{0:T(128)} %copy-done.78) | copy-start | bytes 1540
  130.3 1001.4 %collective-permute-start = (bf16[128,6272]{1,0:T(8,128)(2,1)}, bf16[128,6272]{1,0:T(8,128)(2,1)}, u32[]{:S(2)}, u32[]{:S(2)}) collective-permute-start(bf16[128,6272]{1,0:T(8,128)(2,1)} %copy.565), channel_id=1, source_target_pairs={{0,16},{1,17},{2,18},{3,19},{4,20},{5,21},{6,22},{7,23},{8,24},{9,... | collective-permute-start | bytes 4816904 | tf_op jit(solution)/shard_map/ppermute | solution.py:21
  627.7 1693.7 %reduce-scatter.17.cloned.1.call-start = ((), (), s32[]{:S(2)}) async-start(), calls=%async_computation.13 | async-start | bytes 786432 | tf_op jit(solution)/shard_map/reduce_scatter | solution.py:221
  715.1 1004.9 %collective-permute-start.2 = (bf16[128,6272]{1,0:T(8,128)(2,1)}, bf16[128,6272]{1,0:T(8,128)(2,1)}, u32[]{:S(2)}, u32[]{:S(2)}) collective-permute-start(bf16[128,6272]{1,0:T(8,128)(2,1)} %copy.584), channel_id=1, source_target_pairs={{0,16},{1,17},{2,18},{3,19},{4,20},{5,21},{6,22},{7,23},{8,24},{9,... | collective-permute-start | bytes 4816904 | tf_op jit(solution)/shard_map/ppermute | solution.py:21
  1141.9 1263.4 %reduce-scatter.25.cloned.1.call-start = ((), (), s32[]{:S(2)}) async-start(), calls=%async_computation.18 | async-start | bytes 786432 | tf_op jit(solution)/shard_map/reduce_scatter | solution.py:221
  1149.7 1075.8 %collective-permute-start.3 = (bf16[128,6272]{1,0:T(8,128)(2,1)}, bf16[128,6272]{1,0:T(8,128)(2,1)S(1)}, u32[]{:S(2)}, u32[]{:S(2)}) collective-permute-start(bf16[128,6272]{1,0:T(8,128)(2,1)} %copy.593), channel_id=1, source_target_pairs={{0,16},{1,17},{2,18},{3,19},{4,20},{5,21},{6,22},{7,23},{8,24},{9,... | collective-permute-start | bytes 4816904 | tf_op jit(solution)/shard_map/ppermute | solution.py:21
  1720.0 515.9 %copy-start.108 = (f32[32,2]{0,1:T(2,128)S(1)}, f32[32,2]{0,1:T(2,128)}, u32[]{:S(2)}) copy-start(f32[32,2]{0,1:T(2,128)} %param.112) | copy-start | bytes 772
  1729.4 575.3 %copy-start.107 = (s32[512]{0:T(512)S(1)}, s32[512]{0:T(512)}, u32[]{:S(2)}) copy-start(s32[512]{0:T(512)} %param.106) | copy-start | bytes 6148
  1729.4 590.6 %copy-start.40 = (f32[32,401]{1,0:T(8,128)S(1)}, f32[32,401]{1,0:T(8,128)}, u32[]{:S(2)}) copy-start(f32[32,401]{1,0:T(8,128)} %param.111) | copy-start | bytes 153988
  1729.4 591.3 %copy-start.103 = (s32[512]{0:T(512)S(1)}, s32[512]{0:T(512)}, u32[]{:S(2)}) copy-start(s32[512]{0:T(512)} %param.105) | copy-start | bytes 6148
  1729.4 681.8 %copy-start.104 = (f32[401]{0:T(512)S(1)}, f32[401]{0:T(512)}, u32[]{:S(2)}) copy-start(f32[401]{0:T(512)} %param.113) | copy-start | bytes 4816
  1730.2 678.4 %reduce-scatter.29.cloned.1.call-start = ((), (), s32[]{:S(2)}) async-start(), calls=%async_computation.20 | async-start | bytes 786432 | tf_op jit(solution)/shard_map/reduce_scatter | solution.py:221
  2235.2 176.0 %reduce-scatter.23.cloned.1.call-start = ((), (), s32[]{:S(2)}) async-start(), calls=%async_computation.17 | async-start | bytes 393216 | tf_op jit(solution)/shard_map/reduce_scatter | solution.py:226
  2304.7 108.2 %reduce-scatter.19.cloned.1.call-start = ((), (), s32[]{:S(2)}) async-start(), calls=%async_computation.15 | async-start | bytes 393216 | tf_op jit(solution)/shard_map/reduce_scatter | solution.py:226
  2323.9 94.9 %reduce-scatter.27.cloned.1.call-start = ((), (), s32[]{:S(2)}) async-start(), calls=%async_computation.19 | async-start | bytes 393216 | tf_op jit(solution)/shard_map/reduce_scatter | solution.py:226
  2407.8 25.6 reduce-scatter.31.cloned.1.call-start
  2411.1 290.8 %reduce-scatter.39.cloned.1.call-start = ((), (), s32[]{:S(2)}) async-start(), calls=%async_computation.26 | async-start | bytes 540672
  2486.3 2935.4 %reduce-scatter.35.cloned.1.call-start = ((), (), s32[]{:S(2)}) async-start(), calls=%async_computation.23 | async-start | bytes 2228224 | tf_op jit(solution)/shard_map/reduce_scatter | solution.py:297
  2493.9 2929.6 %reduce-scatter.37.cloned.1.call-start = ((), (), s32[]{:S(2)}) async-start(), calls=%async_computation.24 | async-start | bytes 2162688 | tf_op jit(solution)/shard_map/reduce_scatter | solution.py:300
  2520.2 2904.8 %reduce-scatter.33.cloned.1.call-start = ((), (), s32[]{:S(2)}) async-start(), calls=%async_computation.22 | async-start | bytes 27295744 | tf_op jit(solution)/shard_map/reduce_scatter | solution.py:296
  2617.2 86.0 %collective-permute-start.6 = (bf16[128,6272]{0,1:T(8,128)(2,1)}, bf16[128,6272]{0,1:T(8,128)(2,1)}, u32[]{:S(2)}, u32[]{:S(2)}) collective-permute-start(bf16[128,6272]{0,1:T(8,128)(2,1)} %copy.610), channel_id=1, source_target_pairs={{16,0},{17,1},{18,2},{19,3},{20,4},{21,5},{22,6},{23,7},{24,8},{25... | collective-permute-start | bytes 4816904 | tf_op jit(solution)/shard_map/ppermute | solution.py:21
  2628.5 78.1 %collective-permute-start.5 = (bf16[128,6272]{0,1:T(8,128)(2,1)}, bf16[128,6272]{0,1:T(8,128)(2,1)}, u32[]{:S(2)}, u32[]{:S(2)}) collective-permute-start(bf16[128,6272]{0,1:T(8,128)(2,1)} %copy.604), channel_id=1, source_target_pairs={{16,0},{17,1},{18,2},{19,3},{20,4},{21,5},{22,6},{23,7},{24,8},{25... | collective-permute-start | bytes 4816904 | tf_op jit(solution)/shard_map/ppermute | solution.py:21
  2640.4 68.3 %collective-permute-start.7 = (bf16[128,6272]{0,1:T(8,128)(2,1)}, bf16[128,6272]{0,1:T(8,128)(2,1)}, u32[]{:S(2)}, u32[]{:S(2)}) collective-permute-start(bf16[128,6272]{0,1:T(8,128)(2,1)} %copy.616), channel_id=1, source_target_pairs={{16,0},{17,1},{18,2},{19,3},{20,4},{21,5},{22,6},{23,7},{24,8},{25... | collective-permute-start | bytes 4816904 | tf_op jit(solution)/shard_map/ppermute | solution.py:21
  2654.7 66.7 %collective-permute-start.4 = (bf16[128,6272]{0,1:T(8,128)(2,1)}, bf16[128,6272]{0,1:T(8,128)(2,1)}, u32[]{:S(2)}, u32[]{:S(2)}) collective-permute-start(bf16[128,6272]{0,1:T(8,128)(2,1)} %copy.598), channel_id=1, source_target_pairs={{16,0},{17,1},{18,2},{19,3},{20,4},{21,5},{22,6},{23,7},{24,8},{25... | collective-permute-start | bytes 4816904 | tf_op jit(solution)/shard_map/ppermute | solution.py:21
  2722.9 2692.5 %copy-start.95 = (f32[32,2]{0,1:T(2,128)S(1)}, f32[32,2]{0,1:T(2,128)}, u32[]{:S(2)}) copy-start(f32[32,2]{0,1:T(2,128)} %copy.666) | copy-start | bytes 772
  2722.9 2692.5 %copy-start.109 = (f32[32,2]{0,1:T(2,128)S(1)}, f32[32,2]{0,1:T(2,128)}, u32[]{:S(2)}) copy-start(f32[32,2]{0,1:T(2,128)} %param.112) | copy-start | bytes 772
  2722.9 2692.5 %copy-start.110 = (f32[32,2]{0,1:T(2,128)S(1)}, f32[32,2]{0,1:T(2,128)}, u32[]{:S(2)}) copy-start(f32[32,2]{0,1:T(2,128)} %param.122) | copy-start | bytes 772
  2722.9 2692.5 %copy-start.111 = (f32[32,2]{0,1:T(2,128)S(1)}, f32[32,2]{0,1:T(2,128)}, u32[]{:S(2)}) copy-start(f32[32,2]{0,1:T(2,128)} %param.117) | copy-start | bytes 772
  2722.9 2698.8 %copy-start.20 = (f32[512,64]{0,1:T(8,128)S(1)}, f32[512,64]{0,1:T(8,128)}, u32[]{:S(2)}) copy-start(f32[512,64]{0,1:T(8,128)} %param.110) | copy-start | bytes 393220
  2722.9 2698.8 %copy-start.43 = (f32[512,64]{0,1:T(8,128)S(1)}, f32[512,64]{0,1:T(8,128)}, u32[]{:S(2)}) copy-start(f32[512,64]{0,1:T(8,128)} %param.120) | copy-start | bytes 393220
  2722.9 2700.5 %copy-start.41 = (f32[32,401]{1,0:T(8,128)S(1)}, f32[32,401]{1,0:T(8,128)}, u32[]{:S(2)}) copy-start(f32[32,401]{1,0:T(8,128)} %param.111) | copy-start | bytes 153988
  2723.0 2700.5 %copy-start.47 = (f32[32,401]{1,0:T(8,128)S(1)}, f32[32,401]{1,0:T(8,128)}, u32[]{:S(2)}) copy-start(f32[32,401]{1,0:T(8,128)} %param.121) | copy-start | bytes 153988
  5414.1 3.1 collective-permute-start.8
  (89 other events, 6612.3 us)
Sparse Core Ops, SparseCore 0:
  10.8 14.5 all-gather.9
  27.6 103.7 all-gather.5
  134.2 36.0 all-gather.7
  627.8 519.4 reduce-scatter.20
  1150.0 585.3 reduce-scatter.16
  1737.5 502.5 reduce-scatter.24
  2243.1 14.5 reduce-scatter.28
  2304.8 11.1 reduce-scatter.22
  2324.0 18.5 reduce-scatter.18
  2407.9 10.8 reduce-scatter.26
  2421.7 11.6 reduce-scatter.30
  2486.4 142.1 reduce-scatter.38
  2632.8 57.8 reduce-scatter.34
  2692.9 143.6 reduce-scatter.36
  2841.2 244.2 reduce-scatter.32
where the time goes:
time: 5460 us; the launch traced here: 5440 us
  blocking collectives  2920 us (53%)
  waiting for transfers between devices  1980 us (36%)
  other arithmetic  260 us (5%)
  matrix products  152 us (3%)
  local copies, waits for them, and re-layouts  67.4 us (1%)
    unnamed x1, blocking collectives  2690 us
    ppermute x8, waiting for transfers between devices, from_behind(): lax.ppermute(value, axis, [(source, source + steps) for source in range(f...  1970 us
    add x2, other arithmetic, corners(): index = lower.astype(jnp.int32)[..., None] + jnp.arange(2, dtype=jnp.int32)  157 us
  transfers between devices with their start and end apart: 24, of which 7 were waited for; matrix products, arithmetic and copies ran while one was open for 57% of the time, Pallas kernels for 0%

commit v1 on v0

v1 whole, which is shorter than its diff:
```python
import functools
import math

import jax
import jax.numpy as jnp
from jax import lax
from jax.experimental import pallas as pl
from jax.experimental.pallas import tpu as pltpu
from jax.sharding import PartitionSpec as P

CLASSES = 81
BINS = 7
CELLS = BINS * BINS
WINDOW = 24
GROUP = 16
CHAINS = 4
PADDED = 512
MOMENTUM = 0.9
AVERAGE = 0.7
DECAY = 0.0001
SMOOTH = 0.5

F32 = jnp.float32
BF16 = jnp.bfloat16
VMEM_LIMIT = 52 * 2**20


def smem():
    return pl.BlockSpec(memory_space=pltpu.SMEM)


def vmem():
    return pl.BlockSpec(memory_space=pltpu.VMEM)


def limits():
    return pltpu.CompilerParams(vmem_limit_bytes=VMEM_LIMIT)


def level_plan(height, width):
    shapes = [(height >> depth, width >> depth) for depth in range(4)]
    strides = [max(rows, WINDOW) for rows, cols in shapes]
    bases = [0]
    for depth in range(4):
        bases.append(bases[-1] + strides[depth] * shapes[depth][1])
    total = -(-(bases[-1] + 2 * WINDOW) // GROUP) * GROUP
    return shapes, strides, bases[:4], total


def half_starts(shapes):
    starts = [0]
    for rows, cols in shapes:
        starts.append(starts[-1] + rows // 2 * cols)
    return starts


def table_kernel(height, width, place, own, other, table):
    shapes, strides, bases, total = level_plan(height, width)
    starts = half_starts(shapes)
    table[...] = jnp.zeros_like(table)

    def fill(source, bottom):
        for depth, (rows, cols) in enumerate(shapes):
            half = rows // 2

            def column(x, carry, depth=depth, half=half, cols=cols):
                cells = source[pl.ds(starts[depth] + x, half, stride=cols), :]
                table[pl.ds(bases[depth] + x * strides[depth] + bottom * half, half), :] = cells
                return carry

            lax.fori_loop(0, cols, column, 0, unroll=4)

    bottom = place[0]
    fill(own, bottom)
    fill(other, 1 - bottom)


def build_table(place, own, other, height, width):
    total = level_plan(height, width)[3]
    return pl.pallas_call(
        functools.partial(table_kernel, height, width),
        out_shape=jax.ShapeDtypeStruct((total, own.shape[1]), F32),
        in_specs=[smem(), vmem(), vmem()],
        out_specs=vmem(),
        compiler_params=limits(),
        name="build_table",
    )(place, own, other)


def box_parameters(boxes, levels, height, width):
    shapes, strides, bases, total = level_plan(height, width)
    rows = boxes.shape[0]

    def choose(values, kind):
        out = jnp.full((rows,), values[3], kind)
        for depth in range(3):
            out = jnp.where(levels == depth, jnp.asarray(values[depth], kind), out)
        return out

    reach_y = choose([h - 1 for h, w in shapes], F32)
    reach_x = choose([w - 1 for h, w in shapes], F32)
    stride = choose(strides, jnp.int32)
    base = choose(bases, jnp.int32)
    fraction = (
        (
            jnp.arange(BINS, dtype=F32)[:, None]
            + (jnp.arange(2, dtype=F32)[None, :] + 0.5) * 0.5
        )
        / 7.0
    ).reshape(2 * BINS, 1)
    top = (boxes[:, 0] - 0.25 * boxes[:, 2]) * reach_y
    length_y = 0.5 * boxes[:, 2] * reach_y
    left = (boxes[:, 1] - 0.25 * boxes[:, 3]) * reach_x
    length_x = 0.5 * boxes[:, 3] * reach_x
    first = jnp.clip(jnp.floor(top + length_y * fraction[0, 0]), 0.0, reach_y - 1.0)
    points = left[None] + length_x[None] * fraction
    lower = jnp.clip(jnp.floor(points), 0.0, (reach_x - 1.0)[None])
    upper_weight = points - lower
    address = (base + first.astype(jnp.int32))[None] + lower.astype(jnp.int32) * stride[None]
    row_values = jnp.stack([top, length_y, first, reach_y - 1.0])
    return address.reshape(-1), upper_weight.reshape(-1), row_values.reshape(-1), stride


def row_weights(top, length, first, last, index, offset):
    total = None
    for place in (0.25, 0.75):
        points = top + length * ((index + place) / 7.0)
        lower = jnp.minimum(jnp.maximum(jnp.floor(points), 0.0), last)
        upper_weight = points - lower
        distance = offset - (lower - first)
        part = jnp.where(
            distance == 0.0, 1.0 - upper_weight, jnp.where(distance == 1.0, upper_weight, 0.0)
        )
        total = part if total is None else total + part
    return total * 0.25


def crop_kernel(rows, address, weight, row_values, stride, table, out, turned):
    depth = 256
    lane = lax.broadcasted_iota(jnp.int32, (8, depth), 1)
    offset = (lane % WINDOW).astype(F32)
    index = lax.broadcasted_iota(jnp.int32, (8, depth), 0).astype(F32)
    inside = (
        lax.broadcasted_iota(jnp.int32, (8 * BINS, depth), 0) // 8
        == lax.broadcasted_iota(jnp.int32, (8 * BINS, depth), 1) // WINDOW
    )

    def group(step, carry):
        for part in range(GROUP):
            row = step * GROUP + part
            weights = row_weights(
                row_values[row],
                row_values[rows + row],
                row_values[2 * rows + row],
                row_values[3 * rows + row],
                index,
                offset,
            )
            left = jnp.where(inside, jnp.concatenate([weights] * BINS, axis=0), 0.0).astype(BF16)
            step_x = stride[row]
            columns = []
            for k in range(BINS):
                total = None
                for m in range(2):
                    place = address[(2 * k + m) * rows + row]
                    upper = weight[(2 * k + m) * rows + row]
                    first = table[pl.ds(place, WINDOW), :]
                    second = table[pl.ds(place + step_x, WINDOW), :]
                    value = first + upper * (second - first)
                    total = value if total is None else total + value
                columns.append(total)
            columns.append(jnp.zeros((depth - BINS * WINDOW, 128), F32))
            right = jnp.concatenate(columns, axis=0).astype(BF16)
            crop = jnp.dot(left, right, preferred_element_type=F32)
            for k in range(BINS):
                turned[pl.ds(part + k * BINS * GROUP, BINS, stride=GROUP), :] = crop[
                    8 * k : 8 * k + BINS
                ]
        start = pl.multiple_of(step * GROUP, GROUP)
        for cell in range(CELLS):
            out[pl.ds(start, GROUP), cell * 128 : (cell + 1) * 128] = turned[
                cell * GROUP : (cell + 1) * GROUP, :
            ].astype(BF16)
        return carry

    lax.fori_loop(0, rows // GROUP, group, 0)


def crop_forward(parameters, table):
    rows = parameters[3].shape[0]
    return pl.pallas_call(
        functools.partial(crop_kernel, rows),
        out_shape=jax.ShapeDtypeStruct((rows, CELLS * 128), BF16),
        in_specs=[smem()] * 4 + [vmem()],
        out_specs=vmem(),
        scratch_shapes=[pltpu.VMEM((CELLS * GROUP, 128), F32)],
        compiler_params=limits(),
        name="crop_forward",
    )(*parameters, table)


def spread_kernel(
    rows, height, width, place, address, weight, row_values, stride, grad, own, other, turned, half, *tables
):
    shapes, strides, bases, total = level_plan(height, width)
    starts = half_starts(shapes)
    lane = lax.broadcasted_iota(jnp.int32, (WINDOW, 128), 1)
    index = (lane % 8).astype(F32)
    offset = lax.broadcasted_iota(jnp.int32, (WINDOW, 128), 0).astype(F32)
    long_row = lax.broadcasted_iota(jnp.int32, (BINS * WINDOW, 128), 0)
    long_lane = lax.broadcasted_iota(jnp.int32, (BINS * WINDOW, 128), 1)
    inside = (long_row // WINDOW == long_lane // 8) & (long_lane % 8 < BINS)
    for table in tables:
        table[...] = jnp.zeros_like(table)
    turned[pl.ds(CELLS * GROUP, GROUP), :] = jnp.zeros((GROUP, 128), F32)

    def group(step, carry):
        start = pl.multiple_of(step * GROUP, GROUP)
        for cell in range(CELLS):
            turned[cell * GROUP : (cell + 1) * GROUP, :] = grad[
                pl.ds(start, GROUP), cell * 128 : (cell + 1) * 128
            ].astype(F32)
        for head in range(0, GROUP, CHAINS):
            results = []
            for part in range(head, head + CHAINS):
                row = step * GROUP + part
                weights = row_weights(
                    row_values[row],
                    row_values[rows + row],
                    row_values[2 * rows + row],
                    row_values[3 * rows + row],
                    index,
                    offset,
                )
                left = jnp.where(inside, jnp.concatenate([weights] * BINS, axis=0), 0.0).astype(
                    BF16
                )
                pieces = [
                    turned[pl.ds(part + k * BINS * GROUP, 8, stride=GROUP), :] for k in range(BINS)
                ]
                pieces.append(jnp.zeros((128 - 8 * BINS, 128), F32))
                right = jnp.concatenate(pieces, axis=0).astype(BF16)
                results.append(jnp.dot(left, right, preferred_element_type=F32))
            for k in range(BINS):
                for m in range(2):
                    for chain in range(CHAINS):
                        row = step * GROUP + head + chain
                        table = tables[chain]
                        at = address[(2 * k + m) * rows + row]
                        next_at = at + stride[row]
                        value = results[chain][k * WINDOW : (k + 1) * WINDOW]
                        upper = value * weight[(2 * k + m) * rows + row]
                        first = table[pl.ds(at, WINDOW), :] + (value - upper)
                        second = table[pl.ds(next_at, WINDOW), :] + upper
                        table[pl.ds(at, WINDOW), :] = first
                        table[pl.ds(next_at, WINDOW), :] = second
        return carry

    lax.fori_loop(0, rows // GROUP, group, 0)

    def summed(step, carry):
        span = pl.ds(pl.multiple_of(step * GROUP, GROUP), GROUP)
        value = tables[0][span, :]
        for table in tables[1:]:
            value = value + table[span, :]
        tables[0][span, :] = value
        return carry

    lax.fori_loop(0, total // GROUP, summed, 0)

    def collect(target, bottom):
        for depth, (level_rows, cols) in enumerate(shapes):
            count = level_rows // 2

            def column(x, carry, depth=depth, count=count, cols=cols):
                cells = tables[0][pl.ds(bases[depth] + x * strides[depth] + bottom * count, count), :]
                target[pl.ds(starts[depth] + x, count, stride=cols), :] = cells
                return carry

            lax.fori_loop(0, cols, column, 0, unroll=4)

    bottom = place[0]
    collect(own, bottom)
    collect(half, 1 - bottom)
    other[...] = half[...].astype(BF16)


def crop_backward(place, parameters, grad, height, width):
    rows = parameters[3].shape[0]
    shapes, strides, bases, total = level_plan(height, width)
    cells = half_starts(shapes)[-1]
    return pl.pallas_call(
        functools.partial(spread_kernel, rows, height, width),
        out_shape=(
            jax.ShapeDtypeStruct((cells, 128), F32),
            jax.ShapeDtypeStruct((cells, 128), BF16),
        ),
        in_specs=[smem()] * 5 + [vmem()],
        out_specs=(vmem(), vmem()),
        scratch_shapes=[
            pltpu.VMEM(((CELLS + 1) * GROUP, 128), F32),
            pltpu.VMEM((cells, 128), F32),
        ]
        + [pltpu.VMEM((total, 128), F32)] * CHAINS,
        compiler_params=limits(),
        name="crop_backward",
    )(place, *parameters, grad)


def natural_row(cell):
    k, i = divmod(cell, BINS)
    return i * BINS + k


def turn_kernel(weight, out, turned):
    held = weight.shape[0]
    for tile in range(CELLS):
        turned[tile * 128 : (tile + 1) * 128, 0:held] = jnp.transpose(
            weight[:, tile * 128 : (tile + 1) * 128]
        )
    for cell in range(CELLS):
        block = turned[pl.ds(natural_row(cell), 128, stride=CELLS), :]
        out[:, cell * 128 : (cell + 1) * 128] = jnp.transpose(block)[0:held].astype(BF16)


def turn_weight(weight):
    return pl.pallas_call(
        turn_kernel,
        out_shape=jax.ShapeDtypeStruct(weight.shape, BF16),
        in_specs=[vmem()],
        out_specs=vmem(),
        scratch_shapes=[pltpu.VMEM((weight.shape[1], 128), F32)],
        compiler_params=limits(),
        name="turn_weight",
    )(weight)


def renew(weight, moment, average, grad, rate):
    step_value = grad + DECAY * weight
    moment_new = MOMENTUM * moment + step_value
    weight_new = weight - rate * (step_value + MOMENTUM * moment_new)
    average_new = AVERAGE * average + (1.0 - AVERAGE) * weight_new
    return (weight_new, moment_new, average_new)


def renew_kernel(rate, count, *refs):
    terms = refs[:count]
    weight, moment, average, weight_new, moment_new, average_new, turned = refs[count:]
    held = weight.shape[0]
    for cell in range(CELLS):
        span = slice(cell * 128, (cell + 1) * 128)
        grad = terms[0][:, span].astype(F32)
        for term in terms[1:]:
            grad = grad + term[:, span].astype(F32)
        turned[pl.ds(natural_row(cell), 128, stride=CELLS), 0:held] = jnp.transpose(grad)
    for tile in range(CELLS):
        span = slice(tile * 128, (tile + 1) * 128)
        grad = jnp.transpose(turned[span, :])[0:held]
        new = renew(weight[:, span], moment[:, span], average[:, span], grad, rate)
        weight_new[:, span], moment_new[:, span], average_new[:, span] = new


def renew_first(terms, weight, moment, average, rate):
    return pl.pallas_call(
        functools.partial(renew_kernel, rate, len(terms)),
        out_shape=(jax.ShapeDtypeStruct(weight.shape, F32),) * 3,
        in_specs=[vmem()] * (len(terms) + 3),
        out_specs=(vmem(),) * 3,
        scratch_shapes=[pltpu.VMEM((weight.shape[1], 128), F32)],
        compiler_params=limits(),
        name="renew_first",
    )(*terms, weight, moment, average)


def gelu_parts(value):
    root = math.sqrt(2.0 / math.pi)
    square = value * value
    bend = jnp.tanh(root * (value + 0.044715 * square * value))
    half = 0.5 * (1.0 + bend)
    slope = half + 0.5 * value * (1.0 - bend * bend) * (
        root * (1.0 + 3.0 * 0.044715 * square)
    )
    return value * half, slope


def dot(left, right):
    return jnp.dot(left, right, preferred_element_type=F32)


def dot_last(left, right):
    return lax.dot_general(left, right, (((1,), (1,)), ((), ())), preferred_element_type=F32)


def middle_kernel(
    blocks,
    order,
    pre_own,
    pre_other,
    biases,
    second_turned,
    second,
    out_turned,
    out_weight,
    out_bias,
    slots,
    grad_own,
    grad_other,
    act_first,
    act_second,
    grad_second,
    grad_logits,
    losses,
    pre_first,
    slope_first,
    slope_second,
    grad_first,
):
    hidden, rows = pre_first.shape
    half = hidden // 2
    size = half // blocks
    own_start = order[blocks] * half
    other_start = (1 - order[blocks]) * half
    for block in range(blocks):
        span = slice(block * size, (block + 1) * size)
        at = pl.multiple_of(own_start + order[block] * size, size)
        pre_first[pl.ds(at, size), :] = pre_own[span, :]
        at = pl.multiple_of(other_start + order[block] * size, size)
        pre_first[pl.ds(at, size), :] = pre_other[span, :]
    act, slope = gelu_parts(pre_first[...] + biases[:, 0:1])
    slope_first[...] = slope
    act_first[...] = act.astype(BF16)
    pre_second = dot(second_turned[...], act_first[...]) + biases[:, 1:2]
    act, slope = gelu_parts(pre_second)
    slope_second[...] = slope
    act_second[...] = act.astype(BF16)
    logits = dot(out_turned[...], act_second[...]) + out_bias[...]

    row = lax.broadcasted_iota(jnp.int32, logits.shape, 0)
    live = slots[0:1, :]
    scale = slots[1:2, :]
    chosen = slots[2:3, :].astype(jnp.int32)
    foreground = jnp.where(chosen > 0, 1.0, 0.0)
    is_score = row < CLASSES
    top = jnp.max(jnp.where(is_score, logits, -jnp.inf), axis=0, keepdims=True)
    power = jnp.where(is_score, jnp.exp(logits - top), 0.0)
    total = jnp.sum(power, axis=0, keepdims=True)
    matches = row == chosen
    picked = jnp.sum(jnp.where(matches, logits, 0.0), axis=0, keepdims=True)
    value = jnp.log(total) + top - picked
    grad = power / total - jnp.where(matches, 1.0, 0.0)
    delta_row = CLASSES + 4 * (chosen - 1)
    smooth_total = jnp.zeros_like(live)
    for part in range(4):
        mine = (row == delta_row + part) & (chosen > 0)
        offset = jnp.sum(jnp.where(mine, logits, 0.0), axis=0, keepdims=True) - slots[
            3 + part : 4 + part, :
        ]
        size_of = jnp.abs(offset)
        near = size_of < SMOOTH
        smooth_total = smooth_total + jnp.where(
            near, 0.5 * offset * offset / SMOOTH, size_of - 0.5 * SMOOTH
        )
        slope = jnp.where(near, offset / SMOOTH, jnp.where(offset > 0.0, 1.0, -1.0))
        grad = jnp.where(mine, slope, grad)
    losses[...] = live * (value + foreground * smooth_total)
    grad_logits[...] = (grad * (live * scale)).astype(BF16)
    grad_second[...] = (dot(out_weight[...], grad_logits[...]) * slope_second[...]).astype(BF16)
    grad_first[...] = dot(second[...], grad_second[...]) * slope_first[...]
    for block in range(blocks):
        span = slice(block * size, (block + 1) * size)
        at = pl.multiple_of(own_start + order[block] * size, size)
        grad_own[span, :] = grad_first[pl.ds(at, size), :].astype(BF16)
        at = pl.multiple_of(other_start + order[block] * size, size)
        grad_other[span, :] = grad_first[pl.ds(at, size), :].astype(BF16)


def middle(blocks, order, pre_own, pre_other, biases, second_turned, second, out_turned, out_weight, out_bias, slots):
    half, rows = pre_own.shape
    hidden = 2 * half
    low = lambda *shape: jax.ShapeDtypeStruct(shape, BF16)
    return pl.pallas_call(
        functools.partial(middle_kernel, blocks),
        out_shape=(
            low(half, rows),
            low(half, rows),
            low(hidden, rows),
            low(hidden, rows),
            low(hidden, rows),
            low(PADDED, rows),
            jax.ShapeDtypeStruct((1, rows), F32),
        ),
        in_specs=[smem()] + [vmem()] * 9,
        out_specs=(vmem(),) * 7,
        scratch_shapes=[pltpu.VMEM((hidden, rows), F32)] * 4,
        compiler_params=limits(),
        name="middle",
    )(order, pre_own, pre_other, biases, second_turned, second, out_turned, out_weight, out_bias, slots)


def small_grads_kernel(
    parts, held, act_first, act_second, grad_second, grad_first, grad_logits, second_out, out_out, bias_out
):
    rows = act_first.shape[1]
    depth = act_first.shape[0] // parts
    for part in range(parts):
        value = dot_last(grad_second[...], act_first[part * depth : (part + 1) * depth, :]).astype(BF16)
        for block in range(value.shape[0] // held):
            start = (block * parts + part) * held
            second_out[start : start + held, :] = value[block * held : (block + 1) * held]
    column = lax.broadcasted_iota(jnp.int32, (rows, PADDED), 1)
    width = 5 * CLASSES - 4
    value = dot_last(act_second[...], grad_logits[...])
    value = value + dot(grad_first[...], jnp.where(column == width, 1.0, 0.0).astype(BF16))
    value = value + dot(grad_second[...], jnp.where(column == width + 1, 1.0, 0.0).astype(BF16))
    out_out[...] = value
    bias_out[...] = jnp.sum(grad_logits[...].astype(F32), axis=1, keepdims=True)


def small_grads(parts, held, act_first, act_second, grad_second, grad_first, grad_logits):
    hidden = act_first.shape[0]
    return pl.pallas_call(
        functools.partial(small_grads_kernel, parts, held),
        out_shape=(
            jax.ShapeDtypeStruct((hidden * parts, hidden // parts), BF16),
            jax.ShapeDtypeStruct((hidden, PADDED), F32),
            jax.ShapeDtypeStruct((PADDED, 1), F32),
        ),
        in_specs=[vmem()] * 5,
        out_specs=(vmem(),) * 3,
        compiler_params=limits(),
        name="small_grads",
    )(act_first, act_second, grad_second, grad_first, grad_logits)


def pair_swap(value, count):
    return lax.ppermute(value, "wide", [(at, at ^ 1) for at in range(count)])


def line_step(value, count):
    return lax.ppermute(value, "wide", [(at, (at + 2) % count) for at in range(count)])


def swap(value, axis):
    return lax.ppermute(value, axis, [(0, 1), (1, 0)])


def gather_ring(shard, count):
    line = count // 2
    pieces = []
    moving = shard
    for step in range(line):
        later = line_step(moving, count) if step < line - 1 else None
        pieces.append(moving)
        pieces.append(pair_swap(moving, count))
        moving = later
    return pieces


def scatter_ring(blocks, count):
    line = count // 2
    moving = None
    for step in list(range(1, line)) + [0]:
        crossed = pair_swap(blocks[2 * step + 1], count)
        terms = [blocks[2 * step], crossed]
        if moving is not None:
            terms.append(moving)
        if step == 0:
            return terms
        total = terms[0].astype(F32)
        for term in terms[1:]:
            total = total + term.astype(F32)
        moving = line_step(total.astype(BF16), count)


def body(
    map_p2,
    map_p3,
    map_p4,
    map_p5,
    boxes,
    levels,
    classes,
    sampled,
    counts,
    targets,
    first_weight,
    second_weight,
    out_weight,
    hidden_bias,
    out_bias,
    first_moment,
    second_moment,
    out_moment,
    hidden_moment,
    bias_moment,
    first_average,
    second_average,
    out_average,
    hidden_average,
    bias_average,
):
    n_section = lax.axis_size("section")
    n_fc = lax.axis_size("fc")
    n_wide = lax.axis_size("wide")
    section = lax.axis_index("section")
    fc = lax.axis_index("fc")
    wide = lax.axis_index("wide")
    everywhere = ("section", "wide", "fc")
    maps = [map_p2, map_p3, map_p4, map_p5]
    channels = map_p2.shape[3]
    height = map_p2.shape[1] * n_section
    width = map_p2.shape[2]
    rows_dev = boxes.shape[0]
    rows_own = rows_dev // (n_section * n_fc)
    held = first_weight.shape[1]
    classes_out = out_weight.shape[1]
    place = section.astype(jnp.int32).reshape(1)

    turned = turn_weight(first_weight.T)
    ring = n_wide <= 16
    if ring:
        pieces = gather_ring(turned, n_wide)
        blocks = n_wide
        line, pair = (wide // 2, wide % 2)
        order = jnp.stack(
            [
                ((line - step) % (n_wide // 2)) * 2 + (pair ^ side)
                for step in range(n_wide // 2)
                for side in range(2)
            ]
            + [section]
        ).astype(jnp.int32)
    else:
        pieces = [lax.all_gather(turned, "wide", axis=0, tiled=True)]
        blocks = 1
        order = jnp.stack([jnp.zeros_like(section), section]).astype(jnp.int32)

    live = ((jnp.arange(rows_dev, dtype=jnp.int32) < counts[0]) & (sampled > 0)).astype(F32)
    live_count = jnp.sum(live)
    high = jnp.floor(live_count / 32.0)
    count_columns = jnp.broadcast_to(
        jnp.stack([high, live_count - 32.0 * high])[None], (out_weight.shape[0], 2)
    )
    small = lax.all_gather(
        jnp.concatenate([out_weight, hidden_bias, count_columns], axis=1).astype(BF16),
        everywhere,
        axis=0,
        tiled=True,
    )
    counted = jnp.sum(small[:, classes_out + 2 : classes_out + 4].astype(F32), axis=0)
    total = (32.0 * counted[0] + counted[1]) / (out_weight.shape[0] * n_section * n_fc)
    w_out = jnp.pad(small[:, :classes_out], ((0, 0), (0, PADDED - classes_out)))
    biases = small[:, classes_out : classes_out + 2].astype(F32)
    w_second = lax.all_gather(
        second_weight.T.astype(BF16), everywhere, axis=0, tiled=True
    ).reshape(-1, n_fc, held, second_weight.shape[0])
    w_second_turned = jnp.transpose(w_second, (0, 2, 1, 3)).reshape(
        -1, n_fc * second_weight.shape[0]
    )
    hidden = w_second_turned.shape[0]
    slot_values = jnp.concatenate(
        [
            live[None],
            classes.astype(F32)[None],
            targets.T,
        ],
        axis=0,
    )

    def own_slots(values, axis):
        start = section * (n_fc * rows_own)
        mine = lax.dynamic_slice_in_dim(values, start + fc * rows_own, rows_own, axis)
        theirs = lax.dynamic_slice_in_dim(values, start + (1 - fc) * rows_own, rows_own, axis)
        return mine, theirs

    boxes_mine, boxes_theirs = own_slots(boxes, 0)
    levels_mine, levels_theirs = own_slots(levels, 0)
    slots_mine = own_slots(slot_values, 1)[0]
    slots_mine = jnp.concatenate(
        [slots_mine[0:1], jnp.full((1, rows_own), 1.0, F32) / total, slots_mine[1:]], axis=0
    )
    slots_mine = jnp.pad(slots_mine, ((0, 1), (0, 0)))

    half_own = jnp.concatenate([level_map.reshape(-1, channels) for level_map in maps], axis=0)
    table = build_table(place, half_own, swap(half_own, "section"), height, width)
    crops_mine = crop_forward(box_parameters(boxes_mine, levels_mine, height, width), table)
    passed_mine = swap(crops_mine, "section")
    crops_theirs = crop_forward(box_parameters(boxes_theirs, levels_theirs, height, width), table)
    passed_theirs = swap(crops_theirs, "section")
    inputs = jnp.concatenate([crops_mine, passed_mine, crops_theirs, passed_theirs], axis=0)
    rows_fc = n_section * rows_own

    sums = []
    for piece in pieces:
        term = dot_last(piece, inputs)
        sums.append(term[:, :rows_fc] + swap(term[:, rows_fc:], "fc"))
    pre = jnp.concatenate(sums, axis=0)
    pre_own = pre[:, :rows_own]
    pre_other = swap(pre[:, rows_own:], "section")

    grad_own, grad_other, act_first, act_second, grad_second, grad_logits, losses = middle(
        blocks,
        order,
        pre_own,
        pre_other,
        biases,
        w_second_turned,
        w_second_turned.T,
        w_out.T,
        w_out,
        jnp.pad(out_bias, (0, PADDED - classes_out))[:, None],
        slots_mine,
    )
    grad_mine = jnp.concatenate([grad_own, swap(grad_other, "section")], axis=1)
    grad_all = jnp.concatenate([grad_mine, swap(grad_mine, "fc")], axis=1)

    first_terms = dot(grad_all, inputs).astype(BF16)
    rate = 0.15 * math.sqrt(rows_dev * n_wide)
    if ring:
        first_sums = scatter_ring(
            [first_terms[at * held : (at + 1) * held] for at in range(n_wide)], n_wide
        )
    else:
        first_sums = [lax.psum_scatter(first_terms, "wide", scatter_dimension=0, tiled=True)]

    w_first = jnp.concatenate(pieces, axis=0)
    grad_inputs = lax.dot_general(
        grad_all, w_first, (((0,), (0,)), ((), ())), preferred_element_type=F32
    )
    to_keep = jnp.concatenate(
        [grad_inputs[:rows_own], grad_inputs[rows_fc : rows_fc + rows_own]], axis=0
    )
    to_send = jnp.concatenate(
        [grad_inputs[rows_own:rows_fc], grad_inputs[rows_fc + rows_own :]], axis=0
    ).astype(BF16)
    grad_crops = (to_keep + swap(to_send, "section").astype(F32)).astype(BF16)
    map_own, map_other = crop_backward(
        place,
        box_parameters(
            jnp.concatenate([boxes_mine, boxes_theirs], axis=0),
            jnp.concatenate([levels_mine, levels_theirs], axis=0),
            height,
            width,
        ),
        grad_crops,
        height,
        width,
    )
    own_grad = map_own + swap(map_other, "section").astype(F32)
    map_grads = []
    start_cell = 0
    for level_map in maps:
        cell_count = level_map.shape[1] * level_map.shape[2]
        map_grads.append(own_grad[start_cell : start_cell + cell_count].reshape(level_map.shape))
        start_cell = start_cell + cell_count

    half = hidden // n_section
    first_bias_rows = jnp.concatenate([grad_own, grad_other], axis=0)
    size = half // blocks
    unordered = jnp.zeros_like(first_bias_rows)
    for block in range(blocks):
        for side, where in ((0, section), (1, 1 - section)):
            unordered = lax.dynamic_update_slice_in_dim(
                unordered,
                first_bias_rows[side * half + block * size : side * half + (block + 1) * size],
                where * half + order[block] * size,
                0,
            )
    second_terms, out_terms, bias_terms = small_grads(
        n_fc, held, act_first, act_second, grad_second, unordered, grad_logits
    )
    second_sum = lax.psum_scatter(second_terms, everywhere, scatter_dimension=0, tiled=True)
    out_sum = lax.psum_scatter(out_terms, everywhere, scatter_dimension=0, tiled=True)
    vector = jnp.concatenate([bias_terms[:classes_out, 0], jnp.sum(losses).reshape(1)])
    vector = lax.psum(vector, everywhere)

    first_out = renew_first(first_sums, first_weight.T, first_moment.T, first_average.T, rate)
    second_out = renew(
        second_weight, second_moment, second_average, second_sum.astype(F32).T, rate
    )
    out_out = renew(out_weight, out_moment, out_average, out_sum[:, :classes_out], rate)
    hidden_out = renew(
        hidden_bias,
        hidden_moment,
        hidden_average,
        out_sum[:, classes_out : classes_out + 2],
        rate,
    )
    bias_out = renew(out_bias, bias_moment, bias_average, vector[:classes_out], 4.0)
    return (
        vector[classes_out],
        total,
        map_grads[0],
        map_grads[1],
        map_grads[2],
        map_grads[3],
        first_out[0].T,
        first_out[1].T,
        first_out[2].T,
        *second_out,
        *out_out,
        *hidden_out,
        *bias_out,
    )


def solution(mesh):
    maps = P("wide", "section", None, "fc")
    wide_weight = P("fc", ("section", "wide"))
    tall_weight = P(("section", "wide", "fc"), None)
    in_specs = (
        (maps,) * 4
        + (P("wide", None), P("wide"), P("wide"), P("wide"), P("wide"), P("wide", None))
        + (wide_weight, wide_weight, tall_weight, tall_weight, P()) * 3
    )
    out_specs = (
        (P(), P())
        + (maps,) * 4
        + (wide_weight,) * 6
        + (tall_weight,) * 6
        + (P(),) * 3
    )
    return jax.shard_map(body, mesh=mesh, in_specs=in_specs, out_specs=out_specs, check_vma=False)
```

time: 5460 us -> 546 us (0.10)
  blocking collectives: 2920 us -> 118 us
  waiting for transfers between devices: 1980 us -> 193 us
  other arithmetic: 260 us -> 39.6 us
  matrix products: 152 us -> 30 us
  Pallas kernels: 0 us -> 68.6 us
    unnamed x1 -> x0, blocking collectives: 2690 us -> none
    ppermute x8 -> x30, waiting for transfers between devices: 1970 us -> 106 us  [the longest x8 60.3 us: pair_swap(): return lax.ppermute(value, 'wide', [(at, at ^ 1) for at in range(count)])]
    add x6 -> x5, other arithmetic: 198 us -> 3.95 us  [the longest x1 1.73 us: body(): own_grad = map_own + swap(map_other, 'section').astype(F32)]
    all_gather x10 -> x1, blocking collectives: 186 us -> 73.8 us  [body(): lax.all_gather(jnp.concatenate([out_weight, hidden_bias, count_columns],...]
    dot_general x32 -> x10, matrix products: 106 us -> 30 us  [the longest x8 17.4 us: dot_last(): lax.dot_general(left, right, (((1,), (1,)), ((), ())), preferred_element_...]
    reduce_scatter x11 -> x2, waiting for transfers between devices: 16.8 us -> 87.3 us  [the longest x1 87.3 us: body(): lax.psum_scatter(second_terms, everywhere, scatter_dimension=0, tiled=True)]
    pallas_call x0 -> x8, Pallas kernels: none -> 68.6 us  [the longest x1 26.8 us: crop_backward(): pl.pallas_call(functools.partial(spread_kernel, rows, height, width), out...]
  transfers between devices with their start and end apart: 24 -> 33, of which waited for: 7 -> 12; matrix products, arithmetic and copies ran while one was open for 57% -> 20% of each run, Pallas kernels for 0% -> 10%
where the time goes in v1:
time: 546 us; the launch traced here: 544 us
  waiting for transfers between devices  193 us (35%)
  blocking collectives  118 us (22%)
  Pallas kernels  68.6 us (13%)
  local copies, waits for them, and re-layouts  43.9 us (8%)
  other arithmetic  39.6 us (7%)
  starting transfers between devices  31.3 us (6%)
  matrix products  30 us (5%)
  between operations  19 us (3%)
    reduce_scatter x1, waiting for transfers between devices, body(): lax.psum_scatter(second_terms, everywhere, scatter_dimension=0, tiled=True)  87.3 us
    all_gather x1, blocking collectives, body(): lax.all_gather(jnp.concatenate([out_weight, hidden_bias, count_columns],...  73.8 us
    ppermute x8, waiting for transfers between devices, pair_swap(): return lax.ppermute(value, 'wide', [(at, at ^ 1) for at in range(count)])  60.3 us
    psum x1, blocking collectives, body(): vector = lax.psum(vector, everywhere)  44.7 us
    ppermute x6, waiting for transfers between devices, line_step(): lax.ppermute(value, 'wide', [(at, (at + 2) % count) for at in range(count)])  36.3 us
    pallas_call x1, Pallas kernels, crop_backward(): pl.pallas_call(functools.partial(spread_kernel, rows, height, width), out...  26.8 us
    ppermute x16, starting transfers between devices, swap(): return lax.ppermute(value, axis, [(0, 1), (1, 0)])  21.4 us
    dot_general x8, matrix products, dot_last(): lax.dot_general(left, right, (((1,), (1,)), ((), ())), preferred_element_...  17.4 us
  transfers between devices with their start and end apart: 33, of which 12 were waited for; matrix products, arithmetic and copies ran while one was open for 20% of the time, Pallas kernels for 10%

profile of v1, /device:TPU:1, one launch (start us, length us, event | category | flops | bytes accessed | tf_op | source)
XLA Modules:
  0.0 543.7 jit_solution(302545063207733139)
XLA Ops:
  7.3 2.8 turn_weight.1
  10.1 2.2 collective-permute-start.6
  37.4 73.8 %all_gather.6 = bf16[1024,405]{1,0:T(8,128)(2,1)S(1)} all-gather(bf16[32,405]{1,0:T(8,128)(2,1)S(1)} %maximum_maximum_fusion), channel_id=1, replica_groups=mesh['section'=2,'wide'=8,'fc'=2] {'section','wide','fc'}, dimensions={0}, use_global_device_ids=true | all-gather | bytes 855360 | tf_op jit(solution)/shard_map/all_gather | solution.py:644
  115.1 2.7 fusion.40
  117.8 2.3 copy.80.out_turned
  124.4 1.9 slice_convert_fusion.biases
  126.3 5.3 build_table.1.table
  131.6 8.6 %crop_forward.2 = bf16[128,6272]{1,0:T(8,128)(2,1)S(1)} custom-call(s32[1792]{0:T(1024)S(1)} %get-tuple-element.188.address, f32[1792]{0:T(1024)S(1)} %get-tuple-element.186.weight, f32[512]{0:T(512)S(1)} %maximum_bitcast_fusion.1.row_values, s32[128]{0:T(128)S(1)} %get-tuple-element.194.stride, f32[6672,128]{1,0:T(8,128)} %build_table.1.table), custom_call_target="tpu_custom_call" | custom-call | tf_op jit(solution)/shard_map/crop_forward/pallas_call | solution.py:191
  140.6 8.6 %crop_forward.3 = bf16[128,6272]{1,0:T(8,128)(2,1)S(1)} custom-call(s32[1792]{0:T(1024)S(1)} %get-tuple-element.189.address, f32[1792]{0:T(1024)S(1)} %get-tuple-element.187.weight, f32[512]{0:T(512)S(1)} %maximum_bitcast_fusion.2.row_values, s32[128]{0:T(128)S(1)} %get-tuple-element.191.stride, f32[6672,128]{1,0:T(8,128)} %build_table.1.table), custom_call_target="tpu_custom_call" | custom-call | tf_op jit(solution)/shard_map/crop_forward/pallas_call | solution.py:191
  150.8 2.2 constant_dynamic-update-slice_fusion.9
  154.4 17.5 %collective-permute-done.14 = bf16[64,6272]{1,0:T(8,128)(2,1)S(1)} collective-permute-done((bf16[64,6272]{1,0:T(8,128)(2,1)S(1)}, bf16[64,6272]{1,0:T(8,128)(2,1)S(1)}, u32[]{:S(2)}, u32[]{:S(2)}) %collective-permute-start.14) | collective-permute-done | bytes 802848 | tf_op jit(solution)/shard_map/ppermute | solution.py:540
  174.5 2.0 convolution_bitcast_fusion.1
  176.7 10.2 %collective-permute-done.12 = bf16[64,6272]{1,0:T(8,128)(2,1)S(1)} collective-permute-done((bf16[64,6272]{1,0:T(8,128)(2,1)S(1)}, bf16[64,6272]{1,0:T(8,128)(2,1)S(1)}, u32[]{:S(2)}, u32[]{:S(2)}) %collective-permute-start.12) | collective-permute-done | bytes 802848 | tf_op jit(solution)/shard_map/ppermute | solution.py:536
  186.9 2.0 convolution_bitcast_fusion.2
  189.0 2.0 convolution_bitcast_fusion.3
  192.6 2.0 convolution_bitcast_fusion.4
  194.7 2.0 convolution_bitcast_fusion.5
  196.8 3.2 convolution_bitcast_fusion.6
  200.0 2.0 convolution_bitcast_fusion.7
  202.1 2.0 collective-permute-done.16
  204.1 2.0 convolution_bitcast_fusion
  207.7 2.6 collective-permute-done.5
  210.8 3.0 collective-permute-done.7
  214.7 2.2 collective-permute-done.17
  217.0 5.9 %collective-permute-start.18 = (f32[512,128]{1,0:T(8,128)S(1)}, f32[512,128]{1,0:T(8,128)S(1)}, u32[]{:S(2)}, u32[]{:S(2)}) collective-permute-start(f32[512,128]{1,0:T(8,128)S(1)} %get-tuple-element.167), channel_id=1, source_target_pairs={{0,16},{16,0},{1,17},{17,1},{2,18},{18,2},{3,19},{19,3},{4,20},{20... | collective-permute-start | bytes 786440 | tf_op jit(solution)/shard_map/ppermute | solution.py:544
  223.8 3.8 copy.78
  227.6 1.9 copy.92
  229.5 3.9 copy.79
  233.4 6.6 %middle.1 = (bf16[512,128]{1,0:T(8,128)(2,1)S(1)}, bf16[512,128]{1,0:T(8,128)(2,1)S(1)}, bf16[1024,128]{1,0:T(8,128)(2,1)S(1)}, bf16[1024,128]{1,0:T(8,128)(2,1)...) custom-call(s32[9]{0:T(128)S(1)} %stack.85.order, ...), custom_call_target="tpu_custom_call" | custom-call | tf_op jit(solution)/shard_map/middle/pallas_call | solution.py:481
  240.3 3.2 small_grads.1
  243.6 2.1 constant_dynamic-update-slice_fusion.7
  246.7 2.1 constant_dynamic-update-slice_fusion.5
  249.8 2.1 constant_dynamic-update-slice_fusion.3
  254.6 44.7 %psum.7 = f32[402]{0:T(512)S(1)} all-reduce(f32[402]{0:T(512)S(1)} %pad_maximum_fusion.5), channel_id=1, replica_groups=mesh['section'=2,'wide'=8,'fc'=2] {'section','wide','fc'}, use_global_device_ids=true, to_apply=%region_3.4 | all-reduce | flops 402 | bytes 3216 | tf_op jit(solution)/shard_map/psum | solution.py:775
  299.4 6.6 %convolution_convert_fusion = bf16[512,6272]{1,0:T(8,128)(2,1)S(1)} fusion(bf16[512,512]{1,0:T(8,128)(2,1)S(1)} %constant_dynamic-update-slice_fusion, bf16[512,6272]{1,0:T(8,128)(2,1)} %copy-done), kind=kOutput, calls=%fused_computation | convolution fusion | flops 3291545600 | bytes 13369344 | tf_op jit(solution)/shard_map/dot_general | solution.py:387
  306.0 1.7 fusion.38
  310.7 5.9 %fusion.43 = (bf16[512,6272]{1,0:T(8,128)(2,1)S(1)}, f32[512,6272]{1,0:T(8,128)S(1)}) fusion(bf16[512,512]{1,0:T(8,128)(2,1)S(1)} %constant_dynamic-update-slice_fusion, bf16[512,6272]{1,0:T(8,128)(2,1)} %constant_dynamic-update-slice_fusion.3), kind=kOutput, calls=%fused_computation.193 | convolution fusion | flops 3291545600 | bytes 26214400 | tf_op jit(solution)/shard_map/dot_general | solution.py:727
  316.8 32.9 %collective-permute-done.26 = bf16[64,6272]{1,0:T(8,128)(2,1)S(1)} collective-permute-done((bf16[64,6272]{1,0:T(8,128)(2,1)S(1)}, bf16[64,6272]{1,0:T(8,128)(2,1)S(1)}, u32[]{:S(2)}, u32[]{:S(2)}) %collective-permute-start.26) | collective-permute-done | bytes 802848 | tf_op jit(solution)/shard_map/ppermute | solution.py:536
  351.3 3.8 collective-permute-start.21
  355.2 15.3 %collective-permute-done.25 = bf16[64,6272]{1,0:T(8,128)(2,1)S(1)} collective-permute-done((bf16[64,6272]{1,0:T(8,128)(2,1)}, bf16[64,6272]{1,0:T(8,128)(2,1)S(1)}, u32[]{:S(2)}, u32[]{:S(2)}) %collective-permute-start.25) | collective-permute-done | bytes 802848 | tf_op jit(solution)/shard_map/ppermute | solution.py:536
  370.4 1.9 collective-permute-done.27
  374.2 16.9 %collective-permute-done.28 = bf16[64,6272]{1,0:T(8,128)(2,1)S(1)} collective-permute-done((bf16[64,6272]{1,0:T(8,128)(2,1)S(1)}, bf16[64,6272]{1,0:T(8,128)(2,1)S(1)}, u32[]{:S(2)}, u32[]{:S(2)}) %collective-permute-start.28) | collective-permute-done | bytes 802848 | tf_op jit(solution)/shard_map/ppermute | solution.py:540
  393.2 4.1 fusion.grad
  397.4 26.8 %crop_backward.1 = (f32[3060,128]{1,0:T(8,128)}, bf16[3060,128]{1,0:T(8,128)(2,1)S(1)}) custom-call(s32[1]{0:T(128)} %bitcast.8.place, s32[3584]{0:T(1024)S(1)} %multiply_add_fusion.5.address, f32[3584]{0:T(1024)S(1)} %fusion.9.weight, f32[1024]{0:T(1024)S(1)} %bitcast.203, s32[256]{0:T(256)S(1)} %get-tuple-element.180.stride, bf16[256,6272]{1,0:T(8,128)(2,1)} %fusion.grad), custom_call_target="tpu_custom_call" | custom-call | tf_op jit(solution)/shard_map/crop_backward/pallas_call | solution.py:292
  424.2 5.1 collective-permute-start.22
  431.4 6.6 %renew_first.1 = (f32[64,6272]{1,0:T(8,128)}, f32[64,6272]{1,0:T(8,128)}, f32[64,6272]{1,0:T(8,128)}) custom-call(bf16[64,6272]{1,0:T(8,128)(2,1)S(1)} %get-tuple-element.162.refs_0_, bf16[64,6272]{1,0:T(8,128)(2,1)S(1)} %collective-permute-done.23.refs_1_, bf16[64,6272]{1,0:T(8,128)(2,1)} %copy-done.10, f32[64,6272]{1,0:T(8,128)} %bitcast.210, ...), custom_call_target="tpu_custom_call" | custom-call | tf_op jit(solution)/shard_map/renew_first/pallas_call | solution.py:364
  442.3 87.3 %reduce-scatter.3.cloned.1.call-done = bf16[64,512]{1,0:T(8,128)(2,1)} async-done(((bf16[2048,512]{1,0:T(8,128)(2,1)}), bf16[64,512]{1,0:T(8,128)(2,1)}) %reduce-scatter.3.cloned.1.call-update) | async-done | bytes 65552 | tf_op jit(solution)/shard_map/reduce_scatter | solution.py:772
  531.2 1.7 convert_add_fusion
  (242 shorter events, 66.5 us)
Async XLA Ops:
  7.2 216.6 %all-gather.2.cloned.1.call-start = ((), (), s32[]{:S(2)}) async-start(), calls=%async_computation.2 | async-start | bytes 2162688 | tf_op jit(solution)/shard_map/all_gather | solution.py:654
  10.1 116.2 %collective-permute-start.6 = (bf16[64,6272]{1,0:T(8,128)(2,1)S(1)}, bf16[64,6272]{1,0:T(8,128)(2,1)S(1)}, u32[]{:S(2)}, u32[]{:S(2)}) collective-permute-start(bf16[64,6272]{1,0:T(8,128)(2,1)S(1)} %turn_weight.1), channel_id=1, source_target_pairs={{0,4},{2,6},{4,8},{6,10},{8,12},{10,14},{12,0},{14,2},{1,5},{3,7},... | collective-permute-start | bytes 2408456 | tf_op jit(solution)/shard_map/ppermute | solution.py:540
  12.2 138.5 %collective-permute-start.4 = (bf16[64,6272]{1,0:T(8,128)(2,1)S(1)}, bf16[64,6272]{1,0:T(8,128)(2,1)}, u32[]{:S(2)}, u32[]{:S(2)}) collective-permute-start(bf16[64,6272]{1,0:T(8,128)(2,1)S(1)} %turn_weight.1), channel_id=1, source_target_pairs={{0,2},{2,0},{4,6},{6,4},{8,10},{10,8},{12,14},{14,12},{1,3},{3,1},... | collective-permute-start | bytes 2408456 | tf_op jit(solution)/shard_map/ppermute | solution.py:536
  15.0 423.0 %reduce-scatter.5.cloned.1.call-start = ((), (), s32[]{:S(2)}) async-start(), calls=%async_computation.4 | async-start | bytes 2162688 | tf_op jit(solution)/shard_map/reduce_scatter | solution.py:773
  17.4 108.9 %collective-permute-start = (f32[3060,128]{1,0:T(8,128)S(1)}, f32[3060,128]{1,0:T(8,128)}, u32[]{:S(2)}, u32[]{:S(2)}) collective-permute-start(f32[3060,128]{1,0:T(8,128)S(1)} %pad_maximum_fusion.2.own), channel_id=1, source_target_pairs={{0,16},{16,0},{1,17},{17,1},{2,18},{18,2},{3,19},{19,3},{4,20},{20... | collective-permute-start | bytes 4700168 | tf_op jit(solution)/shard_map/ppermute | solution.py:544
  37.4 84.1 %copy-start.23 = (f32[14]{0:T(128)S(1)}, f32[14]{0:T(128)}, u32[]{:S(2)}) copy-start(f32[14]{0:T(128)} %copy-done.22) | copy-start | bytes 172
  37.4 84.1 %copy-start.26 = (f32[128]{0:T(128)S(1)}, f32[128]{0:T(128)}, u32[]{:S(2)}) copy-start(f32[128]{0:T(128)} %get-tuple-element.173) | copy-start | bytes 1540
  126.3 24.2 %collective-permute-start.10 = (bf16[64,6272]{1,0:T(8,128)(2,1)S(1)}, bf16[64,6272]{1,0:T(8,128)(2,1)S(1)}, u32[]{:S(2)}, u32[]{:S(2)}) collective-permute-start(bf16[64,6272]{1,0:T(8,128)(2,1)S(1)} %collective-permute-done.6), channel_id=1, source_target_pairs={{0,4},{2,6},{4,8},{6,10},{8,12},{10,14},{12,0},{14,2},{1,5},{3,7},... | collective-permute-start | bytes 2408456 | tf_op jit(solution)/shard_map/ppermute | solution.py:540
  140.2 32.6 %collective-permute-start.1 = (bf16[128,6272]{1,0:T(8,128)(2,1)S(1)}, bf16[128,6272]{1,0:T(8,128)(2,1)S(1)}, u32[]{:S(2)}, u32[]{:S(2)}) collective-permute-start(bf16[128,6272]{1,0:T(8,128)(2,1)S(1)} %crop_forward.2), channel_id=1, source_target_pairs={{0,16},{16,0},{1,17},{17,1},{2,18},{18,2},{3,19},{19,3},{4,20},{20... | collective-permute-start | bytes 4816904 | tf_op jit(solution)/shard_map/ppermute | solution.py:544
  149.3 23.6 %collective-permute-start.2 = (bf16[128,6272]{1,0:T(8,128)(2,1)S(1)}, bf16[128,6272]{1,0:T(8,128)(2,1)S(1)}, u32[]{:S(2)}, u32[]{:S(2)}) collective-permute-start(bf16[128,6272]{1,0:T(8,128)(2,1)S(1)} %crop_forward.3), channel_id=1, source_target_pairs={{0,16},{16,0},{1,17},{17,1},{2,18},{18,2},{3,19},{19,3},{4,20},{20... | collective-permute-start | bytes 4816904 | tf_op jit(solution)/shard_map/ppermute | solution.py:544
  150.5 42.1 %collective-permute-start.8 = (bf16[64,6272]{1,0:T(8,128)(2,1)S(1)}, bf16[64,6272]{1,0:T(8,128)(2,1)S(1)}, u32[]{:S(2)}, u32[]{:S(2)}) collective-permute-start(bf16[64,6272]{1,0:T(8,128)(2,1)S(1)} %collective-permute-done.6), channel_id=1, source_target_pairs={{0,2},{2,0},{4,6},{6,4},{8,10},{10,8},{12,14},{14,12},{1,3},{3,1},... | collective-permute-start | bytes 2408456 | tf_op jit(solution)/shard_map/ppermute | solution.py:536
  150.5 38.5 %copy-start.3 = (bf16[64,6272]{1,0:T(8,128)(2,1)}, bf16[64,6272]{1,0:T(8,128)(2,1)S(1)}, u32[]{:S(2)}) copy-start(bf16[64,6272]{1,0:T(8,128)(2,1)S(1)} %collective-permute-done.10) | copy-start | bytes 2408452
  150.5 21.5 %collective-permute-start.14 = (bf16[64,6272]{1,0:T(8,128)(2,1)S(1)}, bf16[64,6272]{1,0:T(8,128)(2,1)S(1)}, u32[]{:S(2)}, u32[]{:S(2)}) collective-permute-start(bf16[64,6272]{1,0:T(8,128)(2,1)S(1)} %collective-permute-done.10), channel_id=1, source_target_pairs={{0,4},{2,6},{4,8},{6,10},{8,12},{10,14},{12,0},{14,2},{1,5},{3,7},... | collective-permute-start | bytes 2408456 | tf_op jit(solution)/shard_map/ppermute | solution.py:540
  152.9 33.9 %collective-permute-start.12 = (bf16[64,6272]{1,0:T(8,128)(2,1)S(1)}, bf16[64,6272]{1,0:T(8,128)(2,1)S(1)}, u32[]{:S(2)}, u32[]{:S(2)}) collective-permute-start(bf16[64,6272]{1,0:T(8,128)(2,1)S(1)} %collective-permute-done.10), channel_id=1, source_target_pairs={{0,2},{2,0},{4,6},{6,4},{8,10},{10,8},{12,14},{14,12},{1,3},{3,1},... | collective-permute-start | bytes 2408456 | tf_op jit(solution)/shard_map/ppermute | solution.py:536
  172.0 32.1 %collective-permute-start.16 = (bf16[64,6272]{1,0:T(8,128)(2,1)S(1)}, bf16[64,6272]{1,0:T(8,128)(2,1)S(1)}, u32[]{:S(2)}, u32[]{:S(2)}) collective-permute-start(bf16[64,6272]{1,0:T(8,128)(2,1)S(1)} %collective-permute-done.14), channel_id=1, source_target_pairs={{0,2},{2,0},{4,6},{6,4},{8,10},{10,8},{12,14},{14,12},{1,3},{3,1},... | collective-permute-start | bytes 2408456 | tf_op jit(solution)/shard_map/ppermute | solution.py:536
  176.6 38.1 %collective-permute-start.15 = (f32[64,256]{1,0:T(8,128)S(1)}, f32[64,256]{1,0:T(8,128)S(1)}, u32[]{:S(2)}, u32[]{:S(2)}) collective-permute-start(f32[64,256]{1,0:T(8,128)S(1)} %slice.323), channel_id=1, source_target_pairs={{0,1},{1,0},{2,3},{3,2},{4,5},{5,4},{6,7},{7,6},{8,9},{9,8},{10,11... | collective-permute-start | bytes 196616 | tf_op jit(solution)/shard_map/ppermute | solution.py:544
  188.9 25.8 %collective-permute-start.13 = (f32[64,256]{1,0:T(8,128)S(1)}, f32[64,256]{1,0:T(8,128)S(1)}, u32[]{:S(2)}, u32[]{:S(2)}) collective-permute-start(f32[64,256]{1,0:T(8,128)S(1)} %slice.321), channel_id=1, source_target_pairs={{0,1},{1,0},{2,3},{3,2},{4,5},{5,4},{6,7},{7,6},{8,9},{9,8},{10,11... | collective-permute-start | bytes 196616 | tf_op jit(solution)/shard_map/ppermute | solution.py:544
  191.1 23.6 %collective-permute-start.11 = (f32[64,256]{1,0:T(8,128)S(1)}, f32[64,256]{1,0:T(8,128)S(1)}, u32[]{:S(2)}, u32[]{:S(2)}) collective-permute-start(f32[64,256]{1,0:T(8,128)S(1)} %slice.319), channel_id=1, source_target_pairs={{0,1},{1,0},{2,3},{3,2},{4,5},{5,4},{6,7},{7,6},{8,9},{9,8},{10,11... | collective-permute-start | bytes 196616 | tf_op jit(solution)/shard_map/ppermute | solution.py:544
  194.6 20.0 %collective-permute-start.9 = (f32[64,256]{1,0:T(8,128)S(1)}, f32[64,256]{1,0:T(8,128)S(1)}, u32[]{:S(2)}, u32[]{:S(2)}) collective-permute-start(f32[64,256]{1,0:T(8,128)S(1)} %slice.317), channel_id=1, source_target_pairs={{0,1},{1,0},{2,3},{3,2},{4,5},{5,4},{6,7},{7,6},{8,9},{9,8},{10,11... | collective-permute-start | bytes 196616 | tf_op jit(solution)/shard_map/ppermute | solution.py:544
  204.1 3.1 collective-permute-start.3
  207.2 3.1 collective-permute-start.5
  210.3 3.5 collective-permute-start.7
  213.8 3.1 collective-permute-start.17
  217.0 16.4 %collective-permute-start.18 = (f32[512,128]{1,0:T(8,128)S(1)}, f32[512,128]{1,0:T(8,128)S(1)}, u32[]{:S(2)}, u32[]{:S(2)}) collective-permute-start(f32[512,128]{1,0:T(8,128)S(1)} %get-tuple-element.167), channel_id=1, source_target_pairs={{0,16},{16,0},{1,17},{17,1},{2,18},{18,2},{3,19},{19,3},{4,20},{20... | collective-permute-start | bytes 786440 | tf_op jit(solution)/shard_map/ppermute | solution.py:544
  243.6 286.0 %reduce-scatter.3.cloned.1.call-start = ((), (), s32[]{:S(2)}) async-start(), calls=%async_computation.3 | async-start | bytes 2162688 | tf_op jit(solution)/shard_map/reduce_scatter | solution.py:772
  249.8 2.9 collective-permute-start.19
  252.7 46.7 %collective-permute-start.20 = (bf16[512,256]{1,0:T(8,128)(2,1)S(1)}, bf16[512,256]{1,0:T(8,128)(2,1)S(1)}, u32[]{:S(2)}, u32[]{:S(2)}) collective-permute-start(bf16[512,256]{1,0:T(8,128)(2,1)S(1)} %pad_maximum_fusion.3), channel_id=1, source_target_pairs={{0,1},{1,0},{2,3},{3,2},{4,5},{5,4},{6,7},{7,6},{8,9},{9,8},{10,11... | collective-permute-start | bytes 786440 | tf_op jit(solution)/shard_map/ppermute | solution.py:544
  307.7 66.5 %collective-permute-start.24 = (bf16[64,6272]{1,0:T(8,128)(2,1)S(1)}, bf16[64,6272]{1,0:T(8,128)(2,1)S(1)}, u32[]{:S(2)}, u32[]{:S(2)}) collective-permute-start(bf16[64,6272]{1,0:T(8,128)(2,1)S(1)} %get-tuple-element.158), channel_id=1, source_target_pairs={{0,2},{2,0},{4,6},{6,4},{8,10},{10,8},{12,14},{14,12},{1,3},{3,1},... | collective-permute-start | bytes 2408456 | tf_op jit(solution)/shard_map/ppermute | solution.py:536
  308.1 41.6 %collective-permute-start.26 = (bf16[64,6272]{1,0:T(8,128)(2,1)S(1)}, bf16[64,6272]{1,0:T(8,128)(2,1)S(1)}, u32[]{:S(2)}, u32[]{:S(2)}) collective-permute-start(bf16[64,6272]{1,0:T(8,128)(2,1)S(1)} %get-tuple-element.159), channel_id=1, source_target_pairs={{0,2},{2,0},{4,6},{6,4},{8,10},{10,8},{12,14},{14,12},{1,3},{3,1},... | collective-permute-start | bytes 2408456 | tf_op jit(solution)/shard_map/ppermute | solution.py:536
  309.2 61.2 %collective-permute-start.25 = (bf16[64,6272]{1,0:T(8,128)(2,1)}, bf16[64,6272]{1,0:T(8,128)(2,1)S(1)}, u32[]{:S(2)}, u32[]{:S(2)}) collective-permute-start(bf16[64,6272]{1,0:T(8,128)(2,1)} %get-tuple-element.160), channel_id=1, source_target_pairs={{0,2},{2,0},{4,6},{6,4},{8,10},{10,8},{12,14},{14,12},{1,3},{3,1},... | collective-permute-start | bytes 2408456 | tf_op jit(solution)/shard_map/ppermute | solution.py:536
  309.5 120.9 %collective-permute-start.23 = (bf16[64,6272]{1,0:T(8,128)(2,1)}, bf16[64,6272]{1,0:T(8,128)(2,1)S(1)}, u32[]{:S(2)}, u32[]{:S(2)}) collective-permute-start(bf16[64,6272]{1,0:T(8,128)(2,1)} %get-tuple-element.161), channel_id=1, source_target_pairs={{0,2},{2,0},{4,6},{6,4},{8,10},{10,8},{12,14},{14,12},{1,3},{3,1},... | collective-permute-start | bytes 2408456 | tf_op jit(solution)/shard_map/ppermute | solution.py:536
  351.0 21.3 %collective-permute-start.27 = (bf16[64,6272]{1,0:T(8,128)(2,1)S(1)}, bf16[64,6272]{1,0:T(8,128)(2,1)S(1)}, u32[]{:S(2)}, u32[]{:S(2)}) collective-permute-start(bf16[64,6272]{1,0:T(8,128)(2,1)S(1)} %add_convert_fusion.2), channel_id=1, source_target_pairs={{0,4},{2,6},{4,8},{6,10},{8,12},{10,14},{12,0},{14,2},{1,5},{3,7},... | collective-permute-start | bytes 2408456 | tf_op jit(solution)/shard_map/ppermute | solution.py:540
  351.3 41.9 %collective-permute-start.21 = (bf16[256,6272]{1,0:T(8,128)(2,1)S(1)}, bf16[256,6272]{1,0:T(8,128)(2,1)}, u32[]{:S(2)}, u32[]{:S(2)}) collective-permute-start(bf16[256,6272]{1,0:T(8,128)(2,1)S(1)} %pad_maximum_fusion.1), channel_id=1, source_target_pairs={{0,16},{16,0},{1,17},{17,1},{2,18},{18,2},{3,19},{19,3},{4,20},{20... | collective-permute-start | bytes 9633800 | tf_op jit(solution)/shard_map/ppermute | solution.py:544
  373.7 17.4 %collective-permute-start.28 = (bf16[64,6272]{1,0:T(8,128)(2,1)S(1)}, bf16[64,6272]{1,0:T(8,128)(2,1)S(1)}, u32[]{:S(2)}, u32[]{:S(2)}) collective-permute-start(bf16[64,6272]{1,0:T(8,128)(2,1)S(1)} %add_convert_fusion.1), channel_id=1, source_target_pairs={{0,4},{2,6},{4,8},{6,10},{8,12},{10,14},{12,0},{14,2},{1,5},{3,7},... | collective-permute-start | bytes 2408456 | tf_op jit(solution)/shard_map/ppermute | solution.py:540
  392.5 37.9 %collective-permute-start.29 = (bf16[64,6272]{1,0:T(8,128)(2,1)S(1)}, bf16[64,6272]{1,0:T(8,128)(2,1)S(1)}, u32[]{:S(2)}, u32[]{:S(2)}) collective-permute-start(bf16[64,6272]{1,0:T(8,128)(2,1)S(1)} %add_convert_fusion), channel_id=1, source_target_pairs={{0,4},{2,6},{4,8},{6,10},{8,12},{10,14},{12,0},{14,2},{1,5},{3,7},... | collective-permute-start | bytes 2408456 | tf_op jit(solution)/shard_map/ppermute | solution.py:540
  393.2 36.1 %copy-start.27 = (f32[401]{0:T(512)S(1)}, f32[401]{0:T(512)}, u32[]{:S(2)}) copy-start(f32[401]{0:T(512)} %param.49) | copy-start | bytes 4816
  393.2 36.1 %copy-start.28 = (f32[401]{0:T(512)S(1)}, f32[401]{0:T(512)}, u32[]{:S(2)}) copy-start(f32[401]{0:T(512)} %param.44) | copy-start | bytes 4816
  397.3 40.7 %copy-start.18 = (f32[32,2]{1,0:T(8,128)S(1)}, f32[32,2]{1,0:T(8,128)}, u32[]{:S(2)}) copy-start(f32[32,2]{1,0:T(8,128)} %copy.85) | copy-start | bytes 772
  397.3 40.7 %copy-start.19 = (f32[32,2]{1,0:T(8,128)S(1)}, f32[32,2]{1,0:T(8,128)}, u32[]{:S(2)}) copy-start(f32[32,2]{1,0:T(8,128)} %copy.82) | copy-start | bytes 772
  397.3 40.7 %copy-start.20 = (f32[32,2]{1,0:T(8,128)S(1)}, f32[32,2]{1,0:T(8,128)}, u32[]{:S(2)}) copy-start(f32[32,2]{1,0:T(8,128)} %copy.86) | copy-start | bytes 772
  397.3 40.7 %copy-start.21 = (f32[32,2]{1,0:T(8,128)S(1)}, f32[32,2]{1,0:T(8,128)}, u32[]{:S(2)}) copy-start(f32[32,2]{1,0:T(8,128)} %copy.84) | copy-start | bytes 772
  397.3 43.4 %copy-start.13 = (f32[32,401]{1,0:T(8,128)S(1)}, f32[32,401]{1,0:T(8,128)}, u32[]{:S(2)}) copy-start(f32[32,401]{1,0:T(8,128)} %param.37) | copy-start | bytes 153988
  397.4 43.4 %copy-start.16 = (f32[32,401]{1,0:T(8,128)S(1)}, f32[32,401]{1,0:T(8,128)}, u32[]{:S(2)}) copy-start(f32[32,401]{1,0:T(8,128)} %param.47) | copy-start | bytes 153988
  397.4 43.4 %copy-start.17 = (f32[32,401]{1,0:T(8,128)S(1)}, f32[32,401]{1,0:T(8,128)}, u32[]{:S(2)}) copy-start(f32[32,401]{1,0:T(8,128)} %param.42) | copy-start | bytes 153988
  397.4 132.2 %copy-start.11 = (f32[512,64]{0,1:T(8,128)S(1)}, f32[512,64]{0,1:T(8,128)}, u32[]{:S(2)}) copy-start(f32[512,64]{0,1:T(8,128)} %param.36) | copy-start | bytes 393220
  397.4 132.2 %copy-start.14 = (f32[512,64]{0,1:T(8,128)S(1)}, f32[512,64]{0,1:T(8,128)}, u32[]{:S(2)}) copy-start(f32[512,64]{0,1:T(8,128)} %param.46) | copy-start | bytes 393220
  397.4 132.2 %copy-start.15 = (f32[512,64]{0,1:T(8,128)S(1)}, f32[512,64]{0,1:T(8,128)}, u32[]{:S(2)}) copy-start(f32[512,64]{0,1:T(8,128)} %param.41) | copy-start | bytes 393220
  424.2 107.0 %collective-permute-start.22 = (bf16[3060,128]{1,0:T(8,128)(2,1)S(1)}, bf16[3060,128]{1,0:T(8,128)(2,1)}, u32[]{:S(2)}, u32[]{:S(2)}) collective-permute-start(bf16[3060,128]{1,0:T(8,128)(2,1)S(1)} %get-tuple-element.45), channel_id=1, source_target_pairs={{0,16},{16,0},{1,17},{17,1},{2,18},{18,2},{3,19},{19,3},{4,20},{20... | collective-permute-start | bytes 2350088 | tf_op jit(solution)/shard_map/ppermute | solution.py:544
  (14 other events, 183.4 us)
Sparse Core Ops, SparseCore 0:
  15.1 60.7 all-gather.1
  243.7 143.2 reduce-scatter.4
  389.3 140.1 reduce-scatter.2

commit v2 on v1

--- a/solution.py
+++ b/solution.py
@@ -33,6 +33,12 @@
     return pl.BlockSpec(memory_space=pltpu.VMEM)
 
 
+def lasting(microseconds):
+    return pl.CostEstimate(
+        flops=0, bytes_accessed=int(microseconds * 3.6e6), transcendentals=0
+    )
+
+
 def limits():
     return pltpu.CompilerParams(vmem_limit_bytes=VMEM_LIMIT)
 
@@ -83,6 +89,7 @@
         in_specs=[smem(), vmem(), vmem()],
         out_specs=vmem(),
         compiler_params=limits(),
+        cost_estimate=lasting(5.0),
         name="build_table",
     )(place, own, other)
 
@@ -135,8 +142,13 @@
     return total * 0.25
 
 
-def crop_kernel(rows, address, weight, row_values, stride, table, out, turned):
+def box_rows(row_values, row, all_rows):
+    return [row_values[part * all_rows + row] for part in range(4)]
+
+
+def crop_kernel(rows, first, address, weight, row_values, stride, table, out, turned):
     depth = 256
+    all_rows = stride.shape[0]
     lane = lax.broadcasted_iota(jnp.int32, (8, depth), 1)
     offset = (lane % WINDOW).astype(F32)
     index = lax.broadcasted_iota(jnp.int32, (8, depth), 0).astype(F32)
@@ -147,26 +159,19 @@
 
     def group(step, carry):
         for part in range(GROUP):
-            row = step * GROUP + part
-            weights = row_weights(
-                row_values[row],
-                row_values[rows + row],
-                row_values[2 * rows + row],
-                row_values[3 * rows + row],
-                index,
-                offset,
-            )
+            row = first + step * GROUP + part
+            weights = row_weights(*box_rows(row_values, row, all_rows), index, offset)
             left = jnp.where(inside, jnp.concatenate([weights] * BINS, axis=0), 0.0).astype(BF16)
             step_x = stride[row]
             columns = []
             for k in range(BINS):
                 total = None
                 for m in range(2):
-                    place = address[(2 * k + m) * rows + row]
-                    upper = weight[(2 * k + m) * rows + row]
-                    first = table[pl.ds(place, WINDOW), :]
-                    second = table[pl.ds(place + step_x, WINDOW), :]
-                    value = first + upper * (second - first)
+                    place = address[(2 * k + m) * all_rows + row]
+                    upper = weight[(2 * k + m) * all_rows + row]
+                    near = table[pl.ds(place, WINDOW), :]
+                    far = table[pl.ds(place + step_x, WINDOW), :]
+                    value = near + upper * (far - near)
                     total = value if total is None else total + value
                 columns.append(total)
             columns.append(jnp.zeros((depth - BINS * WINDOW, 128), F32))
@@ -186,24 +191,27 @@
     lax.fori_loop(0, rows // GROUP, group, 0)
 
 
-def crop_forward(parameters, table):
-    rows = parameters[3].shape[0]
+def crop_forward(parameters, table, first, rows):
     return pl.pallas_call(
-        functools.partial(crop_kernel, rows),
+        functools.partial(crop_kernel, rows, first),
         out_shape=jax.ShapeDtypeStruct((rows, CELLS * 128), BF16),
         in_specs=[smem()] * 4 + [vmem()],
         out_specs=vmem(),
         scratch_shapes=[pltpu.VMEM((CELLS * GROUP, 128), F32)],
         compiler_params=limits(),
+        cost_estimate=lasting(0.07 * rows),
         name="crop_forward",
     )(*parameters, table)
 
 
-def spread_kernel(
-    rows, height, width, place, address, weight, row_values, stride, grad, own, other, turned, half, *tables
-):
+def spread_kernel(rows, first, height, width, last, place, address, weight, row_values, stride, keep, passed, *refs):
     shapes, strides, bases, total = level_plan(height, width)
     starts = half_starts(shapes)
+    all_rows = stride.shape[0]
+    if last:
+        before, own, other, turned, half, *tables = refs
+    else:
+        out, turned, *tables = refs
     lane = lax.broadcasted_iota(jnp.int32, (WINDOW, 128), 1)
     index = (lane % 8).astype(F32)
     offset = lax.broadcasted_iota(jnp.int32, (WINDOW, 128), 0).astype(F32)
@@ -217,21 +225,15 @@
     def group(step, carry):
         start = pl.multiple_of(step * GROUP, GROUP)
         for cell in range(CELLS):
-            turned[cell * GROUP : (cell + 1) * GROUP, :] = grad[
-                pl.ds(start, GROUP), cell * 128 : (cell + 1) * 128
-            ].astype(F32)
+            span = slice(cell * 128, (cell + 1) * 128)
+            turned[cell * GROUP : (cell + 1) * GROUP, :] = keep[pl.ds(start, GROUP), span].astype(
+                F32
+            ) + passed[pl.ds(start, GROUP), span].astype(F32)
         for head in range(0, GROUP, CHAINS):
             results = []
             for part in range(head, head + CHAINS):
-                row = step * GROUP + part
-                weights = row_weights(
-                    row_values[row],
-                    row_values[rows + row],
-                    row_values[2 * rows + row],
-                    row_values[3 * rows + row],
-                    index,
-                    offset,
-                )
+                row = first + step * GROUP + part
+                weights = row_weights(*box_rows(row_values, row, all_rows), index, offset)
                 left = jnp.where(inside, jnp.concatenate([weights] * BINS, axis=0), 0.0).astype(
                     BF16
                 )
@@ -244,36 +246,41 @@
             for k in range(BINS):
                 for m in range(2):
                     for chain in range(CHAINS):
-                        row = step * GROUP + head + chain
+                        row = first + step * GROUP + head + chain
                         table = tables[chain]
-                        at = address[(2 * k + m) * rows + row]
+                        at = address[(2 * k + m) * all_rows + row]
                         next_at = at + stride[row]
                         value = results[chain][k * WINDOW : (k + 1) * WINDOW]
-                        upper = value * weight[(2 * k + m) * rows + row]
-                        first = table[pl.ds(at, WINDOW), :] + (value - upper)
-                        second = table[pl.ds(next_at, WINDOW), :] + upper
-                        table[pl.ds(at, WINDOW), :] = first
-                        table[pl.ds(next_at, WINDOW), :] = second
+                        upper = value * weight[(2 * k + m) * all_rows + row]
+                        near = table[pl.ds(at, WINDOW), :] + (value - upper)
+                        far = table[pl.ds(next_at, WINDOW), :] + upper
+                        table[pl.ds(at, WINDOW), :] = near
+                        table[pl.ds(next_at, WINDOW), :] = far
         return carry
 
     lax.fori_loop(0, rows // GROUP, group, 0)
+    result = tables[0] if last else out
 
     def summed(step, carry):
         span = pl.ds(pl.multiple_of(step * GROUP, GROUP), GROUP)
         value = tables[0][span, :]
         for table in tables[1:]:
             value = value + table[span, :]
-        tables[0][span, :] = value
+        if last:
+            value = value + before[span, :]
+        result[span, :] = value
         return carry
 
     lax.fori_loop(0, total // GROUP, summed, 0)
+    if not last:
+        return
 
     def collect(target, bottom):
         for depth, (level_rows, cols) in enumerate(shapes):
             count = level_rows // 2
 
             def column(x, carry, depth=depth, count=count, cols=cols):
-                cells = tables[0][pl.ds(bases[depth] + x * strides[depth] + bottom * count, count), :]
+                cells = result[pl.ds(bases[depth] + x * strides[depth] + bottom * count, count), :]
                 target[pl.ds(starts[depth] + x, count, stride=cols), :] = cells
                 return carry
 
@@ -285,26 +292,32 @@
     other[...] = half[...].astype(BF16)
 
 
-def crop_backward(place, parameters, grad, height, width):
-    rows = parameters[3].shape[0]
+def crop_backward(place, parameters, keep, passed, first, height, width, before=None):
+    rows = keep.shape[0]
     shapes, strides, bases, total = level_plan(height, width)
     cells = half_starts(shapes)[-1]
-    return pl.pallas_call(
-        functools.partial(spread_kernel, rows, height, width),
-        out_shape=(
+    last = before is not None
+    turned = pltpu.VMEM(((CELLS + 1) * GROUP, 128), F32)
+    tables = [pltpu.VMEM((total, 128), F32)] * CHAINS
+    if last:
+        out_shape = (
             jax.ShapeDtypeStruct((cells, 128), F32),
             jax.ShapeDtypeStruct((cells, 128), BF16),
-        ),
-        in_specs=[smem()] * 5 + [vmem()],
-        out_specs=(vmem(), vmem()),
-        scratch_shapes=[
-            pltpu.VMEM(((CELLS + 1) * GROUP, 128), F32),
-            pltpu.VMEM((cells, 128), F32),
-        ]
-        + [pltpu.VMEM((total, 128), F32)] * CHAINS,
+        )
+        scratch = [turned, pltpu.VMEM((cells, 128), F32)] + tables
+    else:
+        out_shape = jax.ShapeDtypeStruct((total, 128), F32)
+        scratch = [turned] + tables
+    return pl.pallas_call(
+        functools.partial(spread_kernel, rows, first, height, width, last),
+        out_shape=out_shape,
+        in_specs=[smem()] * 5 + [vmem()] * (3 if last else 2),
+        out_specs=(vmem(),) * 2 if last else vmem(),
+        scratch_shapes=scratch,
         compiler_params=limits(),
+        cost_estimate=lasting(0.12 * rows),
         name="crop_backward",
-    )(place, *parameters, grad)
+    )(place, *parameters, keep, passed, *([before] if last else []))
 
 
 def natural_row(cell):
@@ -331,6 +344,7 @@
         out_specs=vmem(),
         scratch_shapes=[pltpu.VMEM((weight.shape[1], 128), F32)],
         compiler_params=limits(),
+        cost_estimate=lasting(2.7),
         name="turn_weight",
     )(weight)
 
@@ -368,6 +382,7 @@
         out_specs=(vmem(),) * 3,
         scratch_shapes=[pltpu.VMEM((weight.shape[1], 128), F32)],
         compiler_params=limits(),
+        cost_estimate=lasting(6.5),
         name="renew_first",
     )(*terms, weight, moment, average)
 
@@ -429,7 +444,11 @@
     act, slope = gelu_parts(pre_first[...] + biases[:, 0:1])
     slope_first[...] = slope
     act_first[...] = act.astype(BF16)
-    pre_second = dot(second_turned[...], act_first[...]) + biases[:, 1:2]
+    pre_second = (
+        dot(second_turned[0], act_first[0:half, :])
+        + dot(second_turned[1], act_first[half:hidden, :])
+        + biases[:, 1:2]
+    )
     act, slope = gelu_parts(pre_second)
     slope_second[...] = slope
     act_second[...] = act.astype(BF16)
@@ -493,83 +512,271 @@
         out_specs=(vmem(),) * 7,
         scratch_shapes=[pltpu.VMEM((hidden, rows), F32)] * 4,
         compiler_params=limits(),
+        cost_estimate=lasting(6.5),
         name="middle",
     )(order, pre_own, pre_other, biases, second_turned, second, out_turned, out_weight, out_bias, slots)
 
 
 def small_grads_kernel(
-    parts, held, act_first, act_second, grad_second, grad_first, grad_logits, second_out, out_out, bias_out
+    blocks,
+    order,
+    act_first,
+    act_second,
+    grad_second,
+    grad_own,
+    grad_other,
+    grad_logits,
+    own,
+    other,
+    bias_out,
+    second_sum,
+    out_sum,
 ):
-    rows = act_first.shape[1]
-    depth = act_first.shape[0] // parts
-    for part in range(parts):
-        value = dot_last(grad_second[...], act_first[part * depth : (part + 1) * depth, :]).astype(BF16)
-        for block in range(value.shape[0] // held):
-            start = (block * parts + part) * held
-            second_out[start : start + held, :] = value[block * held : (block + 1) * held]
+    hidden, rows = act_first.shape
+    half = hidden // 2
+    size = half // blocks
+    section, fc = order[blocks], order[blocks + 1]
+    for side in range(2):
+        second_sum[side] = dot_last(
+            grad_second[...], act_first[side * half : (side + 1) * half, :]
+        ).astype(BF16)
+    width = 5 * CLASSES - 4
     column = lax.broadcasted_iota(jnp.int32, (rows, PADDED), 1)
-    width = 5 * CLASSES - 4
     value = dot_last(act_second[...], grad_logits[...])
-    value = value + dot(grad_first[...], jnp.where(column == width, 1.0, 0.0).astype(BF16))
     value = value + dot(grad_second[...], jnp.where(column == width + 1, 1.0, 0.0).astype(BF16))
-    out_out[...] = value
+    out_sum[...] = value
+    ones = jnp.where(column == width, 1.0, 0.0).astype(BF16)
+    for block in range(blocks):
+        span = slice(block * size, (block + 1) * size)
+        for values, where in ((grad_own, section), (grad_other, 1 - section)):
+            at = pl.ds(pl.multiple_of(where * half + order[block] * size, size), size)
+            out_sum[at, :] = out_sum[at, :] + dot(values[span, :], ones)
     bias_out[...] = jnp.sum(grad_logits[...].astype(F32), axis=1, keepdims=True)
-
-
-def small_grads(parts, held, act_first, act_second, grad_second, grad_first, grad_logits):
+    part = size // 2
+    for target, where in ((own, section), (other, 1 - section)):
+        for near in range(2):
+            lane = fc if near == 0 else 1 - fc
+            for block in range(blocks):
+                start = pl.multiple_of(where * half + order[block] * size, size)
+                target[near, block * size : (block + 1) * size, 0:half] = second_sum[
+                    lane, pl.ds(start, size), :
+                ]
+                at = pl.ds(pl.multiple_of(start + lane * part, part), part)
+                for side in range(2):
+                    target[
+                        near,
+                        block * size + side * part : block * size + (side + 1) * part,
+                        half : half + PADDED // 2,
+                    ] = out_sum[at, side * (PADDED // 2) : (side + 1) * (PADDED // 2)].astype(BF16)
+
+
+def small_grads(blocks, order, act_first, act_second, grad_second, grad_own, grad_other, grad_logits):
     hidden = act_first.shape[0]
+    half = hidden // 2
+    low = jax.ShapeDtypeStruct((2, half, half + PADDED // 2), BF16)
     return pl.pallas_call(
-        functools.partial(small_grads_kernel, parts, held),
-        out_shape=(
-            jax.ShapeDtypeStruct((hidden * parts, hidden // parts), BF16),
-            jax.ShapeDtypeStruct((hidden, PADDED), F32),
-            jax.ShapeDtypeStruct((PADDED, 1), F32),
-        ),
-        in_specs=[vmem()] * 5,
+        functools.partial(small_grads_kernel, blocks),
+        out_shape=(low, low, jax.ShapeDtypeStruct((PADDED, 1), F32)),
+        in_specs=[smem()] + [vmem()] * 6,
         out_specs=(vmem(),) * 3,
+        scratch_shapes=[
+            pltpu.VMEM((2, hidden, half), BF16),
+            pltpu.VMEM((hidden, PADDED), F32),
+        ],
         compiler_params=limits(),
+        cost_estimate=lasting(4.0),
         name="small_grads",
-    )(act_first, act_second, grad_second, grad_first, grad_logits)
+    )(order, act_first, act_second, grad_second, grad_own, grad_other, grad_logits)
+
+
+def assemble_kernel(blocks, order, own, other, second_turned, second, out_weight, out_turned):
+    hidden = second.shape[0]
+    half = hidden // 2
+    size = half // blocks
+    part = size // 2
+    section, fc = order[blocks], order[blocks + 1]
+    for source, where in ((own, section), (other, 1 - section)):
+        for near in range(2):
+            lane = fc if near == 0 else 1 - fc
+            for block in range(blocks):
+                start = pl.multiple_of(where * half + order[block] * size, size)
+                second_turned[lane, pl.ds(start, size), :] = source[
+                    near, block * size : (block + 1) * size, 0:half
+                ]
+                at = pl.ds(pl.multiple_of(start + lane * part, part), part)
+                for side in range(2):
+                    out_weight[at, side * (PADDED // 2) : (side + 1) * (PADDED // 2)] = source[
+                        near,
+                        block * size + side * part : block * size + (side + 1) * part,
+                        half : half + PADDED // 2,
+                    ]
+    for side in range(2):
+        second[side * half : (side + 1) * half, :] = jnp.transpose(second_turned[side])
+    out_turned[...] = jnp.transpose(out_weight[...])
+
+
+def assemble(blocks, order, own, other):
+    half = own.shape[1]
+    hidden = 2 * half
+    low = lambda *shape: jax.ShapeDtypeStruct(shape, BF16)
+    return pl.pallas_call(
+        functools.partial(assemble_kernel, blocks),
+        out_shape=(low(2, hidden, half), low(hidden, hidden), low(hidden, PADDED), low(PADDED, hidden)),
+        in_specs=[smem()] + [vmem()] * 2,
+        out_specs=(vmem(),) * 4,
+        compiler_params=limits(),
+        cost_estimate=lasting(5.0),
+        name="assemble",
+    )(order, own, other)
+
+
+def lane_blocks(lanes):
+    for parts in (7, 1):
+        if lanes % (128 * parts) == 0:
+            return parts, lanes // parts
+
+
+def weight_grad_kernel(count, grad, first, second, third, fourth, *outs):
+    inputs = jnp.concatenate([first[...], second[...], third[...], fourth[...]], axis=0)
+    value = dot(grad[...], inputs).astype(BF16)
+    size = value.shape[0] // count
+    for at in range(count):
+        outs[at][...] = value[at * size : (at + 1) * size]
+
+
+def weight_grad(count, grad, inputs):
+    rows, lanes = inputs[0].shape
+    parts, size = lane_blocks(lanes)
+    held = grad.shape[0] // count
+    return pl.pallas_call(
+        functools.partial(weight_grad_kernel, count),
+        out_shape=(jax.ShapeDtypeStruct((held, lanes), BF16),) * count,
+        grid=(parts,),
+        in_specs=[pl.BlockSpec(grad.shape, lambda step: (0, 0))]
+        + [pl.BlockSpec((rows, size), lambda step: (0, step))] * 4,
+        out_specs=(pl.BlockSpec((held, size), lambda step: (0, step)),) * count,
+        compiler_params=limits(),
+        cost_estimate=lasting(2.0 + 0.4 * count),
+        name="weight_grad",
+    )(grad, *inputs)
+
+
+def input_grad_kernel(count, grad, *refs):
+    weight = jnp.concatenate([ref[...] for ref in refs[:count]], axis=0)
+    value = dot(grad[...], weight).astype(BF16)
+    rows = value.shape[0] // 4
+    for at, out in enumerate(refs[count:]):
+        out[...] = value[at * rows : (at + 1) * rows]
+
+
+def input_grad(grad, pieces):
+    lanes = pieces[0].shape[1]
+    parts, size = lane_blocks(lanes)
+    rows = grad.shape[0] // 4
+    return pl.pallas_call(
+        functools.partial(input_grad_kernel, len(pieces)),
+        out_shape=(jax.ShapeDtypeStruct((rows, lanes), BF16),) * 4,
+        grid=(parts,),
+        in_specs=[pl.BlockSpec(grad.shape, lambda step: (0, 0))]
+        + [pl.BlockSpec((piece.shape[0], size), lambda step: (0, step)) for piece in pieces],
+        out_specs=(pl.BlockSpec((rows, size), lambda step: (0, step)),) * 4,
+        compiler_params=limits(),
+        cost_estimate=lasting(5.0),
+        name="input_grad",
+    )(grad, *pieces)
 
 
 def pair_swap(value, count):
     return lax.ppermute(value, "wide", [(at, at ^ 1) for at in range(count)])
 
 
-def line_step(value, count):
-    return lax.ppermute(value, "wide", [(at, (at + 2) % count) for at in range(count)])
+def line_step(value, count, steps=1):
+    return lax.ppermute(value, "wide", [(at, (at + 2 * steps) % count) for at in range(count)])
 
 
 def swap(value, axis):
     return lax.ppermute(value, axis, [(0, 1), (1, 0)])
 
 
+def after(value, *others):
+    return lax.optimization_barrier((value, *others))[0]
+
+
+def add(*terms):
+    total = terms[0].astype(F32)
+    for term in terms[1:]:
+        total = total + term.astype(F32)
+    return total.astype(BF16)
+
+
+def gather_small(piece, count):
+    line = count // 2
+    held = [piece] + [line_step(piece, count, steps) for steps in range(1, line)]
+    held = jnp.concatenate(held, axis=0)
+    plane = jnp.concatenate([held, pair_swap(held, count)], axis=0)
+    own = jnp.stack([plane, swap(plane, "fc")])
+    return own, swap(own, "section")
+
+
+def scatter_small(own, other, count):
+    line = count // 2
+    both = add(own, swap(other, "section"))
+    plane = add(both[0], swap(both[1], "fc"))
+    half = plane.shape[0] // 2
+    held = add(plane[:half], pair_swap(plane[half:], count))
+    size = half // line
+    terms = [held[:size].astype(F32)]
+    for steps in range(1, line):
+        part = held[steps * size : (steps + 1) * size]
+        terms.append(line_step(part, count, -steps).astype(F32))
+    return functools.reduce(jnp.add, terms)
+
+
 def gather_ring(shard, count):
     line = count // 2
-    pieces = []
-    moving = shard
-    for step in range(line):
-        later = line_step(moving, count) if step < line - 1 else None
-        pieces.append(moving)
-        pieces.append(pair_swap(moving, count))
-        moving = later
-    return pieces
-
-
-def scatter_ring(blocks, count):
+    half = shard.shape[0] // 2
+    straight = [shard]
+    crossed = []
+    for step in range(line - 1):
+        straight.append(line_step(straight[step], count))
+        crossed.append(pair_swap(straight[step], count))
+    tail = [
+        pair_swap(straight[-1][:half], count),
+        line_step(crossed[-1][half:], count),
+    ]
+    return straight, crossed, tail
+
+
+def scatter_ring(straight, crossed, count):
     line = count // 2
-    moving = None
-    for step in list(range(1, line)) + [0]:
-        crossed = pair_swap(blocks[2 * step + 1], count)
-        terms = [blocks[2 * step], crossed]
-        if moving is not None:
-            terms.append(moving)
+    half = straight[0].shape[0] // 2
+    tail = line_step(crossed[1][half:], count)
+    head = pair_swap(crossed[1][:half], count)
+    moving = jnp.concatenate(
+        [add(straight[1][:half], head), straight[1][half:]], axis=0
+    )
+    last = head
+    for step in list(range(2, line)) + [0]:
+        block = crossed[step]
+        if step == 2:
+            block = jnp.concatenate([block[:half], add(block[half:], tail)], axis=0)
+        passed = pair_swap(after(block, last), count)
+        last = passed
+        moving = line_step(moving, count)
         if step == 0:
-            return terms
-        total = terms[0].astype(F32)
-        for term in terms[1:]:
-            total = total + term.astype(F32)
-        moving = line_step(total.astype(BF16), count)
+            return [straight[0], passed, moving]
+        moving = add(straight[step], passed, moving)
+
+
+def split_tall(terms, n_wide):
+    sections, places, half, columns = terms.shape
+    held = half // n_wide
+    second = terms[..., : columns - PADDED // 2].reshape(sections, places, n_wide, held, -1)
+    out = terms[..., columns - PADDED // 2 :].reshape(sections, places, 2, half // 2, PADDED // 2)
+    out = jnp.transpose(out, (0, 1, 3, 2, 4)).reshape(sections, half, PADDED)
+    out = out.reshape(sections, n_wide, places, held // places, 2, PADDED // 2)
+    out = jnp.transpose(out, (0, 2, 1, 4, 3, 5)).reshape(sections, places, n_wide, held, -1)
+    return jnp.concatenate([second, out], axis=-1)
 
 
 def body(
@@ -616,85 +823,102 @@
     classes_out = out_weight.shape[1]
     place = section.astype(jnp.int32).reshape(1)
 
-    turned = turn_weight(first_weight.T)
-    ring = n_wide <= 16
-    if ring:
-        pieces = gather_ring(turned, n_wide)
-        blocks = n_wide
-        line, pair = (wide // 2, wide % 2)
-        order = jnp.stack(
-            [
-                ((line - step) % (n_wide // 2)) * 2 + (pair ^ side)
-                for step in range(n_wide // 2)
-                for side in range(2)
-            ]
-            + [section]
-        ).astype(jnp.int32)
-    else:
-        pieces = [lax.all_gather(turned, "wide", axis=0, tiled=True)]
-        blocks = 1
-        order = jnp.stack([jnp.zeros_like(section), section]).astype(jnp.int32)
+    ring = 4 <= n_wide <= 16
+    line = n_wide // 2
+    rows_tall = out_weight.shape[0]
+    rows_fc = n_section * rows_own
 
     live = ((jnp.arange(rows_dev, dtype=jnp.int32) < counts[0]) & (sampled > 0)).astype(F32)
     live_count = jnp.sum(live)
     high = jnp.floor(live_count / 32.0)
     count_columns = jnp.broadcast_to(
-        jnp.stack([high, live_count - 32.0 * high])[None], (out_weight.shape[0], 2)
-    )
-    small = lax.all_gather(
-        jnp.concatenate([out_weight, hidden_bias, count_columns], axis=1).astype(BF16),
-        everywhere,
-        axis=0,
-        tiled=True,
-    )
-    counted = jnp.sum(small[:, classes_out + 2 : classes_out + 4].astype(F32), axis=0)
-    total = (32.0 * counted[0] + counted[1]) / (out_weight.shape[0] * n_section * n_fc)
-    w_out = jnp.pad(small[:, :classes_out], ((0, 0), (0, PADDED - classes_out)))
-    biases = small[:, classes_out : classes_out + 2].astype(F32)
-    w_second = lax.all_gather(
-        second_weight.T.astype(BF16), everywhere, axis=0, tiled=True
-    ).reshape(-1, n_fc, held, second_weight.shape[0])
-    w_second_turned = jnp.transpose(w_second, (0, 2, 1, 3)).reshape(
-        -1, n_fc * second_weight.shape[0]
-    )
-    hidden = w_second_turned.shape[0]
-    slot_values = jnp.concatenate(
-        [
-            live[None],
-            classes.astype(F32)[None],
-            targets.T,
-        ],
-        axis=0,
-    )
+        jnp.stack([high, live_count - 32.0 * high])[None], (rows_tall, 2)
+    )
+    tall = jnp.concatenate([out_weight, hidden_bias, count_columns], axis=1)
+    tall = jnp.pad(tall, ((0, 0), (0, PADDED - tall.shape[1])))
+    tall = jnp.concatenate([tall[:, : PADDED // 2], tall[:, PADDED // 2 :]], axis=0)
+    piece = jnp.concatenate([second_weight.T, tall], axis=1).astype(BF16)
+    if ring:
+        order = jnp.stack(
+            [
+                ((wide // 2 - step) % line) * 2 + ((wide % 2) ^ side)
+                for side in range(2)
+                for step in range(line)
+            ]
+            + [section, fc]
+        ).astype(jnp.int32)
+        blocks = n_wide
+        small_own, small_other = gather_small(piece, n_wide)
+        w_second_turned, w_second, w_out, w_out_turned = assemble(
+            blocks, order, small_own, small_other
+        )
+    else:
+        order = jnp.stack([jnp.zeros_like(section), section, fc]).astype(jnp.int32)
+        blocks = 1
+        small = lax.all_gather(piece, everywhere, axis=0, tiled=True)
+        small = small.reshape(-1, n_fc, held, piece.shape[1])
+        w_second_turned = jnp.transpose(
+            small[..., : second_weight.shape[0]], (1, 0, 2, 3)
+        ).reshape(n_fc, -1, second_weight.shape[0])
+        w_second = jnp.transpose(w_second_turned, (0, 2, 1)).reshape(
+            -1, w_second_turned.shape[1]
+        )
+        w_out = small[..., second_weight.shape[0] :].reshape(-1, 2, rows_tall, PADDED // 2)
+        w_out = jnp.transpose(w_out, (0, 2, 1, 3)).reshape(-1, PADDED)
+        w_out_turned = w_out.T
+    hidden = w_out.shape[0]
+    biases = w_out[:, classes_out : classes_out + 2].astype(F32)
+    counted = jnp.sum(w_out[:, classes_out + 2 : classes_out + 4].astype(F32), axis=0)
+    total = (32.0 * counted[0] + counted[1]) / (rows_tall * n_section * n_fc)
+
+    turned = turn_weight(first_weight.T)
+    if ring:
+        straight, crossed, tail = gather_ring(turned, n_wide)
+    else:
+        straight, crossed, tail = (
+            [lax.all_gather(turned, "wide", axis=0, tiled=True)],
+            [],
+            [],
+        )
+    pieces = straight + crossed + tail
 
     def own_slots(values, axis):
         start = section * (n_fc * rows_own)
         mine = lax.dynamic_slice_in_dim(values, start + fc * rows_own, rows_own, axis)
         theirs = lax.dynamic_slice_in_dim(values, start + (1 - fc) * rows_own, rows_own, axis)
-        return mine, theirs
-
-    boxes_mine, boxes_theirs = own_slots(boxes, 0)
-    levels_mine, levels_theirs = own_slots(levels, 0)
-    slots_mine = own_slots(slot_values, 1)[0]
-    slots_mine = jnp.concatenate(
-        [slots_mine[0:1], jnp.full((1, rows_own), 1.0, F32) / total, slots_mine[1:]], axis=0
-    )
-    slots_mine = jnp.pad(slots_mine, ((0, 1), (0, 0)))
+        return jnp.concatenate([mine, theirs], axis)
+
+    parameters = box_parameters(own_slots(boxes, 0), own_slots(levels, 0), height, width)
+    slot_values = jnp.concatenate([live[None], classes.astype(F32)[None], targets.T], axis=0)
+    slots = own_slots(slot_values, 1)[:, :rows_own]
+    slots = jnp.concatenate(
+        [slots[0:1], jnp.full((1, rows_own), 1.0, F32) / total, slots[1:]], axis=0
+    )
+    slots = jnp.pad(slots, ((0, 1), (0, 0)))
 
     half_own = jnp.concatenate([level_map.reshape(-1, channels) for level_map in maps], axis=0)
     table = build_table(place, half_own, swap(half_own, "section"), height, width)
-    crops_mine = crop_forward(box_parameters(boxes_mine, levels_mine, height, width), table)
+    crops_mine = crop_forward(parameters, table, 0, rows_own)
     passed_mine = swap(crops_mine, "section")
-    crops_theirs = crop_forward(box_parameters(boxes_theirs, levels_theirs, height, width), table)
+    crops_theirs = crop_forward(parameters, table, rows_own, rows_own)
     passed_theirs = swap(crops_theirs, "section")
-    inputs = jnp.concatenate([crops_mine, passed_mine, crops_theirs, passed_theirs], axis=0)
-    rows_fc = n_section * rows_own
-
-    sums = []
-    for piece in pieces:
-        term = dot_last(piece, inputs)
-        sums.append(term[:, :rows_fc] + swap(term[:, rows_fc:], "fc"))
-    pre = jnp.concatenate(sums, axis=0)
+    inputs = [crops_mine, passed_mine, crops_theirs, passed_theirs]
+    inputs_all = jnp.concatenate(inputs, axis=0)
+
+    def first_layer(parts):
+        terms = [dot_last(part, inputs_all) for part in parts]
+        mine = jnp.concatenate([term[:, :rows_fc] for term in terms], axis=0)
+        theirs = jnp.concatenate([term[:, rows_fc:] for term in terms], axis=0)
+        return mine + swap(theirs, "fc")
+
+    if ring:
+        early = first_layer(straight[:-1] + crossed[:-1])
+        late = first_layer([straight[-1], crossed[-1]])
+        end = first_layer(tail)
+        cut = (line - 1) * held
+        pre = jnp.concatenate([early[:cut], late[:held], early[cut:], late[held:], end], axis=0)
+    else:
+        pre = first_layer(pieces)
     pre_own = pre[:, :rows_own]
     pre_other = swap(pre[:, rows_own:], "section")
 
@@ -705,46 +929,53 @@
         pre_other,
         biases,
         w_second_turned,
-        w_second_turned.T,
-        w_out.T,
+        w_second,
+        w_out_turned,
         w_out,
         jnp.pad(out_bias, (0, PADDED - classes_out))[:, None],
-        slots_mine,
+        slots,
     )
     grad_mine = jnp.concatenate([grad_own, swap(grad_other, "section")], axis=1)
-    grad_all = jnp.concatenate([grad_mine, swap(grad_mine, "fc")], axis=1)
-
-    first_terms = dot(grad_all, inputs).astype(BF16)
+
     rate = 0.15 * math.sqrt(rows_dev * n_wide)
     if ring:
+        def all_slots(parts):
+            mine = jnp.concatenate([grad_mine[at * held : (at + 1) * held] for at in parts], axis=0)
+            return jnp.concatenate([mine, swap(mine, "fc")], axis=1)
+
+        first_at = [1, line + 1]
+        rest_at = [at for at in range(n_wide) if at not in first_at]
+        first_grads = all_slots(first_at)
+        rest_grads = all_slots(rest_at)
+        terms = dict(zip(first_at, weight_grad(2, first_grads, inputs)))
+        terms.update(zip(rest_at, weight_grad(len(rest_at), rest_grads, inputs)))
         first_sums = scatter_ring(
-            [first_terms[at * held : (at + 1) * held] for at in range(n_wide)], n_wide
+            [terms[at] for at in range(line)], [terms[line + at] for at in range(line)], n_wide
+        )
+        grad_all = jnp.concatenate(
+            [
+                rest_grads[:held],
+                first_grads[:held],
+                rest_grads[held : (line) * held],
+                first_grads[held:],
+                rest_grads[line * held :],
+            ],
+            axis=0,
         )
     else:
-        first_sums = [lax.psum_scatter(first_terms, "wide", scatter_dimension=0, tiled=True)]
-
-    w_first = jnp.concatenate(pieces, axis=0)
-    grad_inputs = lax.dot_general(
-        grad_all, w_first, (((0,), (0,)), ((), ())), preferred_element_type=F32
-    )
-    to_keep = jnp.concatenate(
-        [grad_inputs[:rows_own], grad_inputs[rows_fc : rows_fc + rows_own]], axis=0
-    )
-    to_send = jnp.concatenate(
-        [grad_inputs[rows_own:rows_fc], grad_inputs[rows_fc + rows_own :]], axis=0
-    ).astype(BF16)
-    grad_crops = (to_keep + swap(to_send, "section").astype(F32)).astype(BF16)
+        grad_all = jnp.concatenate([grad_mine, swap(grad_mine, "fc")], axis=1)
+        first_sums = [
+            lax.psum_scatter(
+                weight_grad(1, grad_all, inputs)[0], "wide", scatter_dimension=0, tiled=True
+            )
+        ]
+
+    keep_mine, send_mine, keep_theirs, send_theirs = input_grad(grad_all.T, pieces)
+    back_mine = swap(send_mine, "section")
+    back_theirs = swap(send_theirs, "section")
+    before = crop_backward(place, parameters, keep_mine, back_mine, 0, height, width)
     map_own, map_other = crop_backward(
-        place,
-        box_parameters(
-            jnp.concatenate([boxes_mine, boxes_theirs], axis=0),
-            jnp.concatenate([levels_mine, levels_theirs], axis=0),
-            height,
-            width,
-        ),
-        grad_crops,
-        height,
-        width,
+        place, parameters, keep_theirs, back_theirs, rows_own, height, width, before
     )
     own_grad = map_own + swap(map_other, "section").astype(F32)
     map_grads = []
@@ -754,36 +985,46 @@
         map_grads.append(own_grad[start_cell : start_cell + cell_count].reshape(level_map.shape))
         start_cell = start_cell + cell_count
 
-    half = hidden // n_section
-    first_bias_rows = jnp.concatenate([grad_own, grad_other], axis=0)
-    size = half // blocks
-    unordered = jnp.zeros_like(first_bias_rows)
-    for block in range(blocks):
-        for side, where in ((0, section), (1, 1 - section)):
-            unordered = lax.dynamic_update_slice_in_dim(
-                unordered,
-                first_bias_rows[side * half + block * size : side * half + (block + 1) * size],
-                where * half + order[block] * size,
-                0,
-            )
-    second_terms, out_terms, bias_terms = small_grads(
-        n_fc, held, act_first, act_second, grad_second, unordered, grad_logits
-    )
-    second_sum = lax.psum_scatter(second_terms, everywhere, scatter_dimension=0, tiled=True)
-    out_sum = lax.psum_scatter(out_terms, everywhere, scatter_dimension=0, tiled=True)
+    terms_own, terms_other, bias_terms = small_grads(
+        blocks, order, act_first, act_second, grad_second, grad_own, grad_other, grad_logits
+    )
+    if ring:
+        small_sum = scatter_small(terms_own, terms_other, n_wide)
+    else:
+        terms = jnp.stack(
+            [jnp.where(section == at, terms_own, terms_other) for at in range(n_section)]
+        )
+        terms = jnp.where(fc == 0, terms, terms[:, ::-1])
+        terms = jnp.transpose(split_tall(terms, n_wide), (0, 2, 1, 3, 4))
+        small_sum = lax.psum_scatter(
+            terms.reshape(-1, terms.shape[-1]), everywhere, scatter_dimension=0, tiled=True
+        ).astype(F32)
+    second_sum = small_sum[:, : second_weight.shape[0]]
+    tall_sum = small_sum[:, second_weight.shape[0] :]
+    tall_sum = jnp.concatenate([tall_sum[:rows_tall], tall_sum[rows_tall:]], axis=1)
     vector = jnp.concatenate([bias_terms[:classes_out, 0], jnp.sum(losses).reshape(1)])
-    vector = lax.psum(vector, everywhere)
+    if ring:
+        vector = jnp.pad(vector, (0, PADDED - vector.shape[0])).reshape(4, 128)
+        for move in (
+            lambda value: swap(value, "section"),
+            lambda value: swap(value, "fc"),
+            lambda value: pair_swap(value, n_wide),
+        ):
+            vector = vector + move(vector)
+        vector = functools.reduce(
+            jnp.add, [vector] + [line_step(vector, n_wide, steps) for steps in range(1, line)]
+        ).reshape(-1)
+    else:
+        vector = lax.psum(vector, everywhere)
 
     first_out = renew_first(first_sums, first_weight.T, first_moment.T, first_average.T, rate)
-    second_out = renew(
-        second_weight, second_moment, second_average, second_sum.astype(F32).T, rate
-    )
-    out_out = renew(out_weight, out_moment, out_average, out_sum[:, :classes_out], rate)
+    second_out = renew(second_weight, second_moment, second_average, second_sum.T, rate)
+    out_out = renew(out_weight, out_moment, out_average, tall_sum[:, :classes_out], rate)
     hidden_out = renew(
         hidden_bias,
         hidden_moment,
         hidden_average,
-        out_sum[:, classes_out : classes_out + 2],
+        tall_sum[:, classes_out : classes_out + 2],
         rate,
     )
     bias_out = renew(out_bias, bias_moment, bias_average, vector[:classes_out], 4.0)

time: 546 us -> 334 us (0.61)
  blocking collectives: 118 us -> 0 us
  waiting for transfers between devices: 193 us -> 79.2 us
  Pallas kernels: 68.6 us -> 108 us
  starting transfers between devices: 31.3 us -> 56.7 us
  local copies, waits for them, and re-layouts: 43.9 us -> 21.6 us
  between operations: 19 us -> 5.96 us
  other arithmetic: 39.6 us -> 33.5 us
    reduce_scatter x2 -> x0, waiting for transfers between devices: 87.3 us -> none  [the longest x1 87.3 us: body(): lax.psum_scatter(second_terms, everywhere, scatter_dimension=0, tiled=True)]
    all_gather x1 -> x0, blocking collectives: 73.8 us -> none  [body(): lax.all_gather(jnp.concatenate([out_weight, hidden_bias, count_columns],...]
    psum x1 -> x0, blocking collectives: 44.7 us -> none  [body(): vector = lax.psum(vector, everywhere)]
    pallas_call x4 -> x9, Pallas kernels: 47.3 us -> 86.7 us  [the longest x2 35.3 us: crop_backward(): pl.pallas_call(functools.partial(spread_kernel, rows, first, height, widt...]
    ppermute x6 -> x17, waiting for transfers between devices: 36.3 us -> 9.65 us  [line_step(): lax.ppermute(value, 'wide', [(at, (at + 2 * steps) % count) for at in ran...]
    ppermute x6 -> x17, starting transfers between devices: 3.18 us -> 19.9 us  [line_step(): lax.ppermute(value, 'wide', [(at, (at + 2 * steps) % count) for at in ran...]
    dot_general x2 -> x0, matrix products: 12.6 us -> none  [the longest x1 6.63 us: dot(): return jnp.dot(left, right, preferred_element_type=F32)]
    unnamed x73 -> x83, local copies, waits for them, and re-layouts: 17.4 us -> 6.71 us
  transfers between devices with their start and end apart: 33 -> 47, of which waited for: 12 -> 11; matrix products, arithmetic and copies ran while one was open for 20% -> 22% of each run, Pallas kernels for 10% -> 27%
where the time goes in v2:
time: 334 us; the launch traced here: 331 us
  Pallas kernels  108 us (32%)
  waiting for transfers between devices  79.2 us (24%)
  starting transfers between devices  56.7 us (17%)
  other arithmetic  33.5 us (10%)
  matrix products  26 us (8%)
  local copies, waits for them, and re-layouts  21.6 us (6%)
  between operations  5.96 us (2%)
    ppermute x11, waiting for transfers between devices, pair_swap(): return lax.ppermute(value, 'wide', [(at, at ^ 1) for at in range(count)])  52.5 us
    pallas_call x2, Pallas kernels, crop_backward(): pl.pallas_call(functools.partial(spread_kernel, rows, first, height, widt...  35.3 us
    ppermute x19, starting transfers between devices, swap(): return lax.ppermute(value, axis, [(0, 1), (1, 0)])  26.3 us
    dot_general x9, matrix products, dot_last(): lax.dot_general(left, right, (((1,), (1,)), ((), ())), preferred_element_...  26 us
    ppermute x17, starting transfers between devices, line_step(): lax.ppermute(value, 'wide', [(at, (at + 2 * steps) % count) for at in ran...  19.9 us
    pallas_call x2, Pallas kernels, crop_forward(): pl.pallas_call(functools.partial(crop_kernel, rows, first), out_shape=jax...  17.8 us
    ppermute x19, waiting for transfers between devices, swap(): return lax.ppermute(value, axis, [(0, 1), (1, 0)])  17 us
    pallas_call x2, Pallas kernels, weight_grad(): pl.pallas_call(functools.partial(weight_grad_kernel, count), out_shape=(j...  15.2 us
  transfers between devices with their start and end apart: 47, of which 11 were waited for; matrix products, arithmetic and copies ran while one was open for 22% of the time, Pallas kernels for 27%

profile of v2, /device:TPU:1, one launch (start us, length us, event | category | flops | bytes accessed | tf_op | source)
XLA Modules:
  0.0 331.3 jit_solution(4468578733525916358)
XLA Ops:
  7.4 2.1 collective-permute-start.15
  9.6 2.3 collective-permute-start.16
  16.9 2.8 turn_weight.1.refs_0_
  20.5 1.7 pad_maximum_fusion.5
  24.4 8.4 %collective-permute-done.18 = bf16[256,768]{1,0:T(8,128)(2,1)} collective-permute-done((bf16[256,768]{1,0:T(8,128)(2,1)}, bf16[256,768]{1,0:T(8,128)(2,1)}, u32[]{:S(2)}, u32[]{:S(2)}) %collective-permute-start.18) | collective-permute-done | bytes 393248 | tf_op jit(solution)/shard_map/ppermute | solution.py:690
  35.4 5.8 %collective-permute-done.3.refs_1_ = bf16[64,6272]{1,0:T(8,128)(2,1)} collective-permute-done((bf16[64,6272]{1,0:T(8,128)(2,1)S(1)}, bf16[64,6272]{1,0:T(8,128)(2,1)}, u32[]{:S(2)}, u32[]{:S(2)}) %collective-permute-start.3) | collective-permute-done | bytes 802848 | tf_op jit(solution)/shard_map/ppermute | solution.py:694
  41.1 10.9 %collective-permute-done.19 = bf16[512,768]{1,0:T(8,128)(2,1)} collective-permute-done((bf16[512,768]{1,0:T(8,128)(2,1)S(1)}, bf16[512,768]{1,0:T(8,128)(2,1)}, u32[]{:S(2)}, u32[]{:S(2)}) %collective-permute-start.19) | collective-permute-done | bytes 786464 | tf_op jit(solution)/shard_map/ppermute | solution.py:698
  52.0 2.4 pad_maximum_fusion.1.own
  54.4 2.0 collective-permute-start.20
  56.5 5.4 %build_table.1.table = f32[6672,128]{1,0:T(8,128)} custom-call(s32[1]{0:T(128)} %bitcast.8.place, f32[3060,128]{1,0:T(8,128)S(1)} %pad_maximum_fusion.2.own, f32[3060,128]{1,0:T(8,128)} %collective-permute-done.other), custom_call_target="tpu_custom_call" | custom-call | bytes 18000000 | tf_op jit(solution)/shard_map/build_table/pallas_call | solution.py:86
  61.9 8.6 %crop_forward.3.third = bf16[128,6272]{1,0:T(8,128)(2,1)S(1)} custom-call(s32[3584]{0:T(1024)S(1)} %multiply_add_fusion.5.address, f32[3584]{0:T(1024)S(1)} %fusion.5.weight, f32[1024]{0:T(1024)S(1)} %bitcast.117, s32[256]{0:T(256)S(1)} %get-tuple-element.216.stride, f32[6672,128]{1,0:T(8,128)} %build_table.1.table), custom_call_target="tpu_custom_call" | custom-call | bytes 32256000 | tf_op jit(solution)/shard_map/crop_forward/pallas_call | solution.py:195
  70.7 9.2 %crop_forward.2.first = bf16[128,6272]{1,0:T(8,128)(2,1)S(1)} custom-call(s32[3584]{0:T(1024)S(1)} %multiply_add_fusion.5.address, f32[3584]{0:T(1024)S(1)} %fusion.5.weight, f32[1024]{0:T(1024)S(1)} %bitcast.118, s32[256]{0:T(256)S(1)} %get-tuple-element.216.stride, f32[6672,128]{1,0:T(8,128)} %build_table.1.table), custom_call_target="tpu_custom_call" | custom-call | bytes 32256000 | tf_op jit(solution)/shard_map/crop_forward/pallas_call | solution.py:195
  82.6 16.8 %collective-permute-done.9.refs_6_ = bf16[64,6272]{1,0:T(8,128)(2,1)} collective-permute-done((bf16[64,6272]{1,0:T(8,128)(2,1)}, bf16[64,6272]{1,0:T(8,128)(2,1)}, u32[]{:S(2)}, u32[]{:S(2)}) %collective-permute-start.9) | collective-permute-done | bytes 802848 | tf_op jit(solution)/shard_map/ppermute | solution.py:690
  100.6 1.8 slice.341
  102.6 1.8 slice.339
  105.5 5.0 %assemble.1 = (bf16[2,1024,512]{2,1,0:T(8,128)(2,1)}, bf16[1024,1024]{1,0:T(8,128)(2,1)}, bf16[1024,512]{1,0:T(8,128)(2,1)S(1)}, bf16[512,1024]{1,0:T(8,128)(2,1)}) custom-call(s32[10]{0:T(128)S(1)} %stack.68.order, bf16[2,512,768]{2,1,0:T(8,128)(2,1)} %pad_maximum_fusion.1.own, bf16[2,512,768]{2,1,0:T(8,128)(2,1)} %collective-permute-done.20.other), custom_call_target="tpu_custom_call" | custom-call | bytes 18000000 | tf_op jit(solution)/shard_map/assemble/pallas_call | solution.py:622
  114.8 3.2 pad_maximum_fusion
  118.0 2.0 convolution_bitcast_fusion.6
  120.1 3.2 convolution_bitcast_fusion.5
  123.3 3.2 convolution_bitcast_fusion.4
  126.5 3.2 convolution_bitcast_fusion.3
  129.7 5.3 %collective-permute-done.6.refs_5_ = bf16[64,6272]{1,0:T(8,128)(2,1)} collective-permute-done((bf16[64,6272]{1,0:T(8,128)(2,1)}, bf16[64,6272]{1,0:T(8,128)(2,1)}, u32[]{:S(2)}, u32[]{:S(2)}) %collective-permute-start.6) | collective-permute-done | bytes 802848 | tf_op jit(solution)/shard_map/ppermute | solution.py:690
  135.0 3.2 convolution_bitcast_fusion.2
  139.5 3.2 convolution_bitcast_fusion
  142.7 3.2 convolution_bitcast_fusion.1
  146.2 2.9 convolution_bitcast_fusion.7
  149.2 2.0 convolution_bitcast_fusion.8
  152.7 2.6 collective-permute-done.13
  155.4 4.8 %collective-permute-start.14 = (f32[512,128]{1,0:T(8,128)S(1)}, f32[512,128]{1,0:T(8,128)S(1)}, u32[]{:S(2)}, u32[]{:S(2)}) collective-permute-start(f32[512,128]{1,0:T(8,128)S(1)} %get-tuple-element.180), channel_id=1, source_target_pairs={{0,16},{16,0},{1,17},{17,1},{2,18},{18,2},{3,19},{19,3},{4,20},{20... | collective-permute-start | bytes 786440 | tf_op jit(solution)/shard_map/ppermute | solution.py:698
  160.3 1.9 slice_convert_fusion.biases
  162.2 6.9 %middle.1 = (bf16[512,128]{1,0:T(8,128)(2,1)S(1)}, bf16[512,128]{1,0:T(8,128)(2,1)S(1)}, bf16[1024,128]{1,0:T(8,128)(2,1)S(1)}, bf16[1024,128]{1,0:T(8,128)(2,1)...) custom-call(s32[10]{0:T(128)S(1)} %stack.68.order, ...), custom_call_target="tpu_custom_call" | custom-call | bytes 23400000 | tf_op jit(solution)/shard_map/middle/pallas_call | solution.py:500
  169.7 4.1 %small_grads.1 = (bf16[2,512,768]{2,1,0:T(8,128)(2,1)}, bf16[2,512,768]{2,1,0:T(8,128)(2,1)}, f32[512,1]{1,0:T(8,128)S(1)}) custom-call(s32[10]{0:T(128)S(1)} %stack.68.order, bf16[1024,128]{1,0:T(8,128)(2,1)S(1)} %get-tuple-element.59.act_first, bf16[1024,128]{1,0:T(8,128)(2,1)S(1)} %get-tuple-element.60.act_second, ...), custom_call_target="tpu_custom_call" | custom-call | bytes 14400000 | tf_op jit(solution)/shard_map/small_grads/pallas_call | solution.py:577
  180.9 1.7 collective-permute-start.41
  182.6 2.9 collective-permute-start.26
  188.8 6.4 %weight_grad.3 = (bf16[64,6272]{1,0:T(8,128)(2,1)S(1)}, bf16[64,6272]{1,0:T(8,128)(2,1)S(1)}) custom-call(bf16[128,512]{1,0:T(8,128)(2,1)S(1)} %pad_maximum_fusion.9.grad, bf16[128,6272]{1,0:T(8,128)(2,1)} %copy-done.1, bf16[128,6272]{1,0:T(8,128)(2,1)} %collective-permute-done.1.second, bf16[128,6272]{1,0:T(8,128)(2,1)} %copy-done, ...), custom_call_target="tpu_custom_call" | custom-call | bytes 10080000 | tf_op jit(solution)/shard_map/weight_grad/pallas_call | solution.py:651
  197.9 8.8 %weight_grad.2 = (bf16[64,6272]{1,0:T(8,128)(2,1)S(1)}, bf16[64,6272]{1,0:T(8,128)(2,1)S(1)}, bf16[64,6272]{1,0:T(8,128)(2,1)}, bf16[64,6272]{1,0:T(8,128)(2,1)}...) custom-call(bf16[384,512]{1,0:T(8,128)(2,1)S(1)} %pad_maximum_fusion.6.grad, bf16[128,6272]{1,0:T(8,128)(2,1)} %copy-done.1, ...), custom_call_target="tpu_custom_call" | custom-call | bytes 15840000 | tf_op jit(solution)/shard_map/weight_grad/pallas_call | solution.py:651
  212.7 2.6 collective-permute-start.38
  217.3 9.3 %input_grad.1 = (bf16[128,6272]{1,0:T(8,128)(2,1)}, bf16[128,6272]{1,0:T(8,128)(2,1)}, bf16[128,6272]{1,0:T(8,128)(2,1)}, bf16[128,6272]{1,0:T(8,128)(2,1)}) custom-call(bf16[512,512]{1,0:T(8,128)(2,1)S(1)} %copy.75.grad, bf16[64,6272]{1,0:T(8,128)(2,1)} %copy-done.2, bf16[64,6272]{1,0:T(8,128)(2,1)} %collective-permute-done.3.refs_1_, ...), custom_call_target="tpu_custom_call" | custom-call | bytes 18000000 | tf_op jit(solution)/shard_map/input_grad/pallas_call | solution.py:676
  228.2 6.0 %collective-permute-start.30 = (bf16[128,6272]{1,0:T(8,128)(2,1)}, bf16[128,6272]{1,0:T(8,128)(2,1)}, u32[]{:S(2)}, u32[]{:S(2)}) collective-permute-start(bf16[128,6272]{1,0:T(8,128)(2,1)} %get-tuple-element.68), channel_id=1, source_target_pairs={{0,16},{16,0},{1,17},{17,1},{2,18},{18,2},{3,19},{19,3},{4,20},{20... | collective-permute-start | bytes 4816904 | tf_op jit(solution)/shard_map/ppermute | solution.py:698
  234.2 1.8 add_convert_fusion
  239.3 2.8 add_convert_fusion.2
  244.3 15.8 %crop_backward.2.refs_0_ = f32[6672,128]{1,0:T(8,128)} custom-call(s32[1]{0:T(128)} %bitcast.8.place, s32[3584]{0:T(1024)S(1)} %multiply_add_fusion.5.address, f32[3584]{0:T(1024)S(1)} %fusion.5.weight, f32[1024]{0:T(1024)S(1)} %bitcast.119, s32[256]{0:T(256)S(1)} %get-tuple-element.216.stride, bf16[128,6272]{1,0:T(8,128)(2,1)S(1)} %copy-done.5, ...), custom_call_target="tpu_custom_call" | custom-call | bytes 55296000 | tf_op jit(solution)/shard_map/crop_backward/pallas_call | solution.py:311
  260.1 19.5 %crop_backward.3 = (f32[3060,128]{1,0:T(8,128)}, bf16[3060,128]{1,0:T(8,128)(2,1)S(1)}) custom-call(s32[1]{0:T(128)} %bitcast.8.place, s32[3584]{0:T(1024)S(1)} %multiply_add_fusion.5.address, f32[3584]{0:T(1024)S(1)} %fusion.5.weight, f32[1024]{0:T(1024)S(1)} %bitcast.120, s32[256]{0:T(256)S(1)} %get-tuple-element.216.stride, ...), custom_call_target="tpu_custom_call" | custom-call | bytes 55296000 | tf_op jit(solution)/shard_map/crop_backward/pallas_call | solution.py:311
  283.9 2.3 add_convert_fusion.1
  287.0 22.0 %collective-permute-done.43 = bf16[256,768]{1,0:T(8,128)(2,1)S(1)} collective-permute-done((bf16[256,768]{1,0:T(8,128)(2,1)S(1)}, bf16[256,768]{1,0:T(8,128)(2,1)S(1)}, u32[]{:S(2)}, u32[]{:S(2)}) %collective-permute-start.43) | collective-permute-done | bytes 393248 | tf_op jit(solution)/shard_map/ppermute | solution.py:690
  310.0 2.7 collective-permute-start.45
  316.1 3.8 %collective-permute-done.45 = bf16[64,768]{1,0:T(8,128)(2,1)S(1)} collective-permute-done((bf16[64,768]{1,0:T(8,128)(2,1)S(1)}, bf16[64,768]{1,0:T(8,128)(2,1)S(1)}, u32[]{:S(2)}, u32[]{:S(2)}) %collective-permute-start.45) | collective-permute-done | bytes 98336 | tf_op jit(solution)/shard_map/ppermute | solution.py:694
  323.5 6.6 %renew_first.1 = (f32[64,6272]{1,0:T(8,128)}, f32[64,6272]{1,0:T(8,128)}, f32[64,6272]{1,0:T(8,128)}) custom-call(bf16[64,6272]{1,0:T(8,128)(2,1)S(1)} %get-tuple-element.73.refs_0_, bf16[64,6272]{1,0:T(8,128)(2,1)S(1)} %collective-permute-done.37.refs_1_, bf16[64,6272]{1,0:T(8,128)(2,1)} %collective-permute-done.40.refs_2_, f32[64,6272]{1,0:T(8,128)} %bitcast.122, ...), custom_call_target="tpu_custom_call" | custom-call | bytes 23400000 | tf_op jit(solution)/shard_map/renew_first/pallas_call | solution.py:378
  (271 shorter events, 68.6 us)
Async XLA Ops:
  7.4 13.0 %collective-permute-start.15 = (bf16[64,768]{1,0:T(8,128)(2,1)}, bf16[64,768]{1,0:T(8,128)(2,1)S(1)}, u32[]{:S(2)}, u32[]{:S(2)}) collective-permute-start(bf16[64,768]{1,0:T(8,128)(2,1)} %get-tuple-element.204), channel_id=1, source_target_pairs={{0,4},{2,6},{4,8},{6,10},{8,12},{10,14},{12,0},{14,2},{1,5},{3,7},... | collective-permute-start | bytes 294920 | tf_op jit(solution)/shard_map/ppermute | solution.py:694
  9.6 10.9 %collective-permute-start.16 = (bf16[64,768]{1,0:T(8,128)(2,1)}, bf16[64,768]{1,0:T(8,128)(2,1)S(1)}, u32[]{:S(2)}, u32[]{:S(2)}) collective-permute-start(bf16[64,768]{1,0:T(8,128)(2,1)} %get-tuple-element.204), channel_id=1, source_target_pairs={{0,8},{2,10},{4,12},{6,14},{8,0},{10,2},{12,4},{14,6},{1,9},{3,11}... | collective-permute-start | bytes 294920 | tf_op jit(solution)/shard_map/ppermute | solution.py:694
  11.9 8.6 %collective-permute-start.17 = (bf16[64,768]{1,0:T(8,128)(2,1)}, bf16[64,768]{1,0:T(8,128)(2,1)}, u32[]{:S(2)}, u32[]{:S(2)}) collective-permute-start(bf16[64,768]{1,0:T(8,128)(2,1)} %get-tuple-element.204), channel_id=1, source_target_pairs={{0,12},{2,14},{4,0},{6,2},{8,4},{10,6},{12,8},{14,10},{1,13},{3,15... | collective-permute-start | bytes 294920 | tf_op jit(solution)/shard_map/ppermute | solution.py:694
  15.3 41.2 %collective-permute-start = (f32[3060,128]{1,0:T(8,128)S(1)}, f32[3060,128]{1,0:T(8,128)}, u32[]{:S(2)}, u32[]{:S(2)}) collective-permute-start(f32[3060,128]{1,0:T(8,128)S(1)} %pad_maximum_fusion.2.own), channel_id=1, source_target_pairs={{0,16},{16,0},{1,17},{17,1},{2,18},{18,2},{3,19},{19,3},{4,20},{20... | collective-permute-start | bytes 4700168 | tf_op jit(solution)/shard_map/ppermute | solution.py:698
  19.7 21.5 %collective-permute-start.3 = (bf16[64,6272]{1,0:T(8,128)(2,1)S(1)}, bf16[64,6272]{1,0:T(8,128)(2,1)}, u32[]{:S(2)}, u32[]{:S(2)}) collective-permute-start(bf16[64,6272]{1,0:T(8,128)(2,1)S(1)} %turn_weight.1.refs_0_), channel_id=1, source_target_pairs={{0,4},{2,6},{4,8},{6,10},{8,12},{10,14},{12,0},{14,2},{1,5},{3,7},... | collective-permute-start | bytes 2408456 | tf_op jit(solution)/shard_map/ppermute | solution.py:694
  22.2 10.7 %collective-permute-start.18 = (bf16[256,768]{1,0:T(8,128)(2,1)}, bf16[256,768]{1,0:T(8,128)(2,1)}, u32[]{:S(2)}, u32[]{:S(2)}) collective-permute-start(bf16[256,768]{1,0:T(8,128)(2,1)} %pad_maximum_fusion.5), channel_id=1, source_target_pairs={{0,2},{2,0},{4,6},{6,4},{8,10},{10,8},{12,14},{14,12},{1,3},{3,1},... | collective-permute-start | bytes 1179656 | tf_op jit(solution)/shard_map/ppermute | solution.py:690
  33.9 18.1 %collective-permute-start.19 = (bf16[512,768]{1,0:T(8,128)(2,1)S(1)}, bf16[512,768]{1,0:T(8,128)(2,1)}, u32[]{:S(2)}, u32[]{:S(2)}) collective-permute-start(bf16[512,768]{1,0:T(8,128)(2,1)S(1)} %constant_dynamic-update-slice_fusion), channel_id=1, source_target_pairs={{0,1},{1,0},{2,3},{3,2},{4,5},{5,4},{6,7},{7,6},{8,9},{9,8},{10,11... | collective-permute-start | bytes 2359304 | tf_op jit(solution)/shard_map/ppermute | solution.py:698
  41.1 38.8 %collective-permute-start.4 = (bf16[64,6272]{1,0:T(8,128)(2,1)}, bf16[64,6272]{1,0:T(8,128)(2,1)}, u32[]{:S(2)}, u32[]{:S(2)}) collective-permute-start(bf16[64,6272]{1,0:T(8,128)(2,1)} %collective-permute-done.3.refs_1_), channel_id=1, source_target_pairs={{0,4},{2,6},{4,8},{6,10},{8,12},{10,14},{12,0},{14,2},{1,5},{3,7},... | collective-permute-start | bytes 2408456 | tf_op jit(solution)/shard_map/ppermute | solution.py:694
  54.4 50.0 %collective-permute-start.20 = (bf16[2,512,768]{2,1,0:T(8,128)(2,1)}, bf16[2,512,768]{2,1,0:T(8,128)(2,1)}, u32[]{:S(2)}, u32[]{:S(2)}) collective-permute-start(bf16[2,512,768]{2,1,0:T(8,128)(2,1)} %pad_maximum_fusion.1.own), channel_id=1, source_target_pairs={{0,16},{16,0},{1,17},{17,1},{2,18},{18,2},{3,19},{19,3},{4,20},{20... | collective-permute-start | bytes 4718600 | tf_op jit(solution)/shard_map/ppermute | solution.py:698
  70.5 44.3 %copy-start = (bf16[128,6272]{1,0:T(8,128)(2,1)}, bf16[128,6272]{1,0:T(8,128)(2,1)S(1)}, u32[]{:S(2)}) copy-start(bf16[128,6272]{1,0:T(8,128)(2,1)S(1)} %crop_forward.3.third) | copy-start | bytes 4816900
  70.6 43.0 %collective-permute-start.2 = (bf16[128,6272]{1,0:T(8,128)(2,1)S(1)}, bf16[128,6272]{1,0:T(8,128)(2,1)}, u32[]{:S(2)}, u32[]{:S(2)}) collective-permute-start(bf16[128,6272]{1,0:T(8,128)(2,1)S(1)} %crop_forward.3.third), channel_id=1, source_target_pairs={{0,16},{16,0},{1,17},{17,1},{2,18},{18,2},{3,19},{19,3},{4,20},{20... | collective-permute-start | bytes 4816904 | tf_op jit(solution)/shard_map/ppermute | solution.py:698
  79.9 35.0 %collective-permute-start.1 = (bf16[128,6272]{1,0:T(8,128)(2,1)S(1)}, bf16[128,6272]{1,0:T(8,128)(2,1)}, u32[]{:S(2)}, u32[]{:S(2)}) collective-permute-start(bf16[128,6272]{1,0:T(8,128)(2,1)S(1)} %crop_forward.2.first), channel_id=1, source_target_pairs={{0,16},{16,0},{1,17},{17,1},{2,18},{18,2},{3,19},{19,3},{4,20},{20... | collective-permute-start | bytes 4816904 | tf_op jit(solution)/shard_map/ppermute | solution.py:698
  79.9 19.4 %collective-permute-start.9 = (bf16[64,6272]{1,0:T(8,128)(2,1)}, bf16[64,6272]{1,0:T(8,128)(2,1)}, u32[]{:S(2)}, u32[]{:S(2)}) collective-permute-start(bf16[64,6272]{1,0:T(8,128)(2,1)} %collective-permute-done.4.refs_2_), channel_id=1, source_target_pairs={{0,2},{2,0},{4,6},{6,4},{8,10},{10,8},{12,14},{14,12},{1,3},{3,1},... | collective-permute-start | bytes 2408456 | tf_op jit(solution)/shard_map/ppermute | solution.py:690
  81.2 21.1 %collective-permute-start.8 = (bf16[64,6272]{1,0:T(8,128)(2,1)}, bf16[64,6272]{1,0:T(8,128)(2,1)}, u32[]{:S(2)}, u32[]{:S(2)}) collective-permute-start(bf16[64,6272]{1,0:T(8,128)(2,1)} %collective-permute-done.4.refs_2_), channel_id=1, source_target_pairs={{0,4},{2,6},{4,8},{6,10},{8,12},{10,14},{12,0},{14,2},{1,5},{3,7},... | collective-permute-start | bytes 2408456 | tf_op jit(solution)/shard_map/ppermute | solution.py:694
  99.4 27.1 %collective-permute-start.5 = (bf16[64,6272]{1,0:T(8,128)(2,1)}, bf16[64,6272]{1,0:T(8,128)(2,1)}, u32[]{:S(2)}, u32[]{:S(2)}) collective-permute-start(bf16[64,6272]{1,0:T(8,128)(2,1)} %copy-done.2), channel_id=1, source_target_pairs={{0,2},{2,0},{4,6},{6,4},{8,10},{10,8},{12,14},{14,12},{1,3},{3,1},... | collective-permute-start | bytes 2408456 | tf_op jit(solution)/shard_map/ppermute | solution.py:690
  102.4 32.6 %collective-permute-start.6 = (bf16[64,6272]{1,0:T(8,128)(2,1)}, bf16[64,6272]{1,0:T(8,128)(2,1)}, u32[]{:S(2)}, u32[]{:S(2)}) collective-permute-start(bf16[64,6272]{1,0:T(8,128)(2,1)} %collective-permute-done.3.refs_1_), channel_id=1, source_target_pairs={{0,2},{2,0},{4,6},{6,4},{8,10},{10,8},{12,14},{14,12},{1,3},{3,1},... | collective-permute-start | bytes 2408456 | tf_op jit(solution)/shard_map/ppermute | solution.py:690
  104.4 41.8 %collective-permute-start.12 = (bf16[32,6272]{1,0:T(8,128)(2,1)}, bf16[32,6272]{1,0:T(8,128)(2,1)}, u32[]{:S(2)}, u32[]{:S(2)}) collective-permute-start(bf16[32,6272]{1,0:T(8,128)(2,1)} %slice.341), channel_id=1, source_target_pairs={{0,4},{2,6},{4,8},{6,10},{8,12},{10,14},{12,0},{14,2},{1,5},{3,7},... | collective-permute-start | bytes 1204232 | tf_op jit(solution)/shard_map/ppermute | solution.py:694
  113.6 35.6 %collective-permute-start.11 = (bf16[32,6272]{1,0:T(8,128)(2,1)}, bf16[32,6272]{1,0:T(8,128)(2,1)S(1)}, u32[]{:S(2)}, u32[]{:S(2)}) collective-permute-start(bf16[32,6272]{1,0:T(8,128)(2,1)} %slice.339), channel_id=1, source_target_pairs={{0,2},{2,0},{4,6},{6,4},{8,10},{10,8},{12,14},{14,12},{1,3},{3,1},... | collective-permute-start | bytes 1204232 | tf_op jit(solution)/shard_map/ppermute | solution.py:690
  138.2 14.4 %collective-permute-start.7 = (f32[320,256]{1,0:T(8,128)S(1)}, f32[320,256]{1,0:T(8,128)S(1)}, u32[]{:S(2)}, u32[]{:S(2)}) collective-permute-start(f32[320,256]{1,0:T(8,128)S(1)} %get-tuple-element.194), channel_id=1, source_target_pairs={{0,1},{1,0},{2,3},{3,2},{4,5},{5,4},{6,7},{7,6},{8,9},{9,8},{10,11... | collective-permute-start | bytes 983048 | tf_op jit(solution)/shard_map/ppermute | solution.py:698
  145.9 6.6 %collective-permute-start.10 = (f32[128,256]{1,0:T(8,128)S(1)}, f32[128,256]{1,0:T(8,128)S(1)}, u32[]{:S(2)}, u32[]{:S(2)}) collective-permute-start(f32[128,256]{1,0:T(8,128)S(1)} %pad_maximum_fusion.8), channel_id=1, source_target_pairs={{0,1},{1,0},{2,3},{3,2},{4,5},{5,4},{6,7},{7,6},{8,9},{9,8},{10,11... | collective-permute-start | bytes 393224 | tf_op jit(solution)/shard_map/ppermute | solution.py:698
  151.2 4.1 %collective-permute-start.13 = (f32[64,256]{1,0:T(8,128)S(1)}, f32[64,256]{1,0:T(8,128)S(1)}, u32[]{:S(2)}, u32[]{:S(2)}) collective-permute-start(f32[64,256]{1,0:T(8,128)S(1)} %pad_maximum_fusion.12), channel_id=1, source_target_pairs={{0,1},{1,0},{2,3},{3,2},{4,5},{5,4},{6,7},{7,6},{8,9},{9,8},{10,11... | collective-permute-start | bytes 196616 | tf_op jit(solution)/shard_map/ppermute | solution.py:698
  155.4 6.8 %collective-permute-start.14 = (f32[512,128]{1,0:T(8,128)S(1)}, f32[512,128]{1,0:T(8,128)S(1)}, u32[]{:S(2)}, u32[]{:S(2)}) collective-permute-start(f32[512,128]{1,0:T(8,128)S(1)} %get-tuple-element.180), channel_id=1, source_target_pairs={{0,16},{16,0},{1,17},{17,1},{2,18},{18,2},{3,19},{19,3},{4,20},{20... | collective-permute-start | bytes 786440 | tf_op jit(solution)/shard_map/ppermute | solution.py:698
  174.6 1.2 collective-permute-start.21
  176.5 2.4 collective-permute-start.22
  177.7 7.7 %collective-permute-start.27 = (bf16[512,128]{1,0:T(8,128)(2,1)S(1)}, bf16[512,128]{1,0:T(8,128)(2,1)S(1)}, u32[]{:S(2)}, u32[]{:S(2)}) collective-permute-start(bf16[512,128]{1,0:T(8,128)(2,1)S(1)} %get-tuple-element.63.grad_other), channel_id=1, source_target_pairs={{0,16},{16,0},{1,17},{17,1},{2,18},{18,2},{3,19},{19,3},{4,20},{20... | collective-permute-start | bytes 393224 | tf_op jit(solution)/shard_map/ppermute | solution.py:698
  179.7 2.9 collective-permute-start.23
  180.9 47.3 %collective-permute-start.41 = (bf16[2,512,768]{2,1,0:T(8,128)(2,1)}, bf16[2,512,768]{2,1,0:T(8,128)(2,1)}, u32[]{:S(2)}, u32[]{:S(2)}) collective-permute-start(bf16[2,512,768]{2,1,0:T(8,128)(2,1)} %get-tuple-element.88), channel_id=1, source_target_pairs={{0,16},{16,0},{1,17},{17,1},{2,18},{18,2},{3,19},{19,3},{4,20},{20... | collective-permute-start | bytes 4718600 | tf_op jit(solution)/shard_map/ppermute | solution.py:698
  182.6 54.4 %collective-permute-start.26 = (f32[4,128]{1,0:T(4,128)S(1)}, f32[4,128]{1,0:T(4,128)S(1)}, u32[]{:S(2)}, u32[]{:S(2)}) collective-permute-start(f32[4,128]{1,0:T(4,128)S(1)} %add.340), channel_id=1, source_target_pairs={{0,12},{2,14},{4,0},{6,2},{8,4},{10,6},{12,8},{14,10},{1,13},{3,15... | collective-permute-start | bytes 6152 | tf_op jit(solution)/shard_map/ppermute | solution.py:694
  185.5 51.5 %collective-permute-start.25 = (f32[4,128]{1,0:T(4,128)S(1)}, f32[4,128]{1,0:T(4,128)S(1)}, u32[]{:S(2)}, u32[]{:S(2)}) collective-permute-start(f32[4,128]{1,0:T(4,128)S(1)} %add.340), channel_id=1, source_target_pairs={{0,8},{2,10},{4,12},{6,14},{8,0},{10,2},{12,4},{14,6},{1,9},{3,11}... | collective-permute-start | bytes 6152 | tf_op jit(solution)/shard_map/ppermute | solution.py:694
  185.6 3.2 collective-permute-start.29
  186.9 8.8 %collective-permute-start.28 = (bf16[384,256]{1,0:T(8,128)(2,1)S(1)}, bf16[384,256]{1,0:T(8,128)(2,1)S(1)}, u32[]{:S(2)}, u32[]{:S(2)}) collective-permute-start(bf16[384,256]{1,0:T(8,128)(2,1)S(1)} %pad_maximum_fusion.7), channel_id=1, source_target_pairs={{0,1},{1,0},{2,3},{3,2},{4,5},{5,4},{6,7},{7,6},{8,9},{9,8},{10,11... | collective-permute-start | bytes 589832 | tf_op jit(solution)/shard_map/ppermute | solution.py:698
  195.3 13.8 %collective-permute-start.33 = (bf16[32,6272]{1,0:T(8,128)(2,1)S(1)}, bf16[32,6272]{1,0:T(8,128)(2,1)S(1)}, u32[]{:S(2)}, u32[]{:S(2)}) collective-permute-start(bf16[32,6272]{1,0:T(8,128)(2,1)S(1)} %get-tuple-element.179), channel_id=1, source_target_pairs={{0,4},{2,6},{4,8},{6,10},{8,12},{10,14},{12,0},{14,2},{1,5},{3,7},... | collective-permute-start | bytes 1204232 | tf_op jit(solution)/shard_map/ppermute | solution.py:694
  195.7 15.4 %collective-permute-start.34 = (bf16[32,6272]{1,0:T(8,128)(2,1)S(1)}, bf16[32,6272]{1,0:T(8,128)(2,1)S(1)}, u32[]{:S(2)}, u32[]{:S(2)}) collective-permute-start(bf16[32,6272]{1,0:T(8,128)(2,1)S(1)} %get-tuple-element.178), channel_id=1, source_target_pairs={{0,2},{2,0},{4,6},{6,4},{8,10},{10,8},{12,14},{14,12},{1,3},{3,1},... | collective-permute-start | bytes 1204232 | tf_op jit(solution)/shard_map/ppermute | solution.py:690
  211.1 15.5 %collective-permute-start.35 = (bf16[64,6272]{1,0:T(8,128)(2,1)}, bf16[64,6272]{1,0:T(8,128)(2,1)}, u32[]{:S(2)}, u32[]{:S(2)}) collective-permute-start(bf16[64,6272]{1,0:T(8,128)(2,1)} %pad_maximum_fusion.3), channel_id=1, source_target_pairs={{0,2},{2,0},{4,6},{6,4},{8,10},{10,8},{12,14},{14,12},{1,3},{3,1},... | collective-permute-start | bytes 2408456 | tf_op jit(solution)/shard_map/ppermute | solution.py:690
  212.7 25.3 %collective-permute-start.38 = (bf16[64,6272]{1,0:T(8,128)(2,1)}, bf16[64,6272]{1,0:T(8,128)(2,1)}, u32[]{:S(2)}, u32[]{:S(2)}) collective-permute-start(bf16[64,6272]{1,0:T(8,128)(2,1)} %pad_maximum_fusion.4), channel_id=1, source_target_pairs={{0,4},{2,6},{4,8},{6,10},{8,12},{10,14},{12,0},{14,2},{1,5},{3,7},... | collective-permute-start | bytes 2408456 | tf_op jit(solution)/shard_map/ppermute | solution.py:694
  226.6 15.5 %collective-permute-start.24 = (f32[4,128]{1,0:T(4,128)S(1)}, f32[4,128]{1,0:T(4,128)S(1)}, u32[]{:S(2)}, u32[]{:S(2)}) collective-permute-start(f32[4,128]{1,0:T(4,128)S(1)} %add.340), channel_id=1, source_target_pairs={{0,4},{2,6},{4,8},{6,10},{8,12},{10,14},{12,0},{14,2},{1,5},{3,7},... | collective-permute-start | bytes 6152 | tf_op jit(solution)/shard_map/ppermute | solution.py:694
  228.2 31.9 %collective-permute-start.30 = (bf16[128,6272]{1,0:T(8,128)(2,1)}, bf16[128,6272]{1,0:T(8,128)(2,1)}, u32[]{:S(2)}, u32[]{:S(2)}) collective-permute-start(bf16[128,6272]{1,0:T(8,128)(2,1)} %get-tuple-element.68), channel_id=1, source_target_pairs={{0,16},{16,0},{1,17},{17,1},{2,18},{18,2},{3,19},{19,3},{4,20},{20... | collective-permute-start | bytes 4816904 | tf_op jit(solution)/shard_map/ppermute | solution.py:698
  237.0 7.3 %collective-permute-start.31 = (bf16[128,6272]{1,0:T(8,128)(2,1)}, bf16[128,6272]{1,0:T(8,128)(2,1)}, u32[]{:S(2)}, u32[]{:S(2)}) collective-permute-start(bf16[128,6272]{1,0:T(8,128)(2,1)} %get-tuple-element.70), channel_id=1, source_target_pairs={{0,16},{16,0},{1,17},{17,1},{2,18},{18,2},{3,19},{19,3},{4,20},{20... | collective-permute-start | bytes 4816904 | tf_op jit(solution)/shard_map/ppermute | solution.py:698
  237.0 44.0 %collective-permute-start.36 = (bf16[64,6272]{1,0:T(8,128)(2,1)}, bf16[64,6272]{1,0:T(8,128)(2,1)}, u32[]{:S(2)}, u32[]{:S(2)}) collective-permute-start(bf16[64,6272]{1,0:T(8,128)(2,1)} %get-tuple-element.79), channel_id=1, source_target_pairs={{0,2},{2,0},{4,6},{6,4},{8,10},{10,8},{12,14},{14,12},{1,3},{3,1},... | collective-permute-start | bytes 2408456 | tf_op jit(solution)/shard_map/ppermute | solution.py:690
  238.1 43.3 %collective-permute-start.42 = (bf16[512,768]{1,0:T(8,128)(2,1)}, bf16[512,768]{1,0:T(8,128)(2,1)}, u32[]{:S(2)}, u32[]{:S(2)}) collective-permute-start(bf16[512,768]{1,0:T(8,128)(2,1)} %slice_bitcast_fusion), channel_id=1, source_target_pairs={{0,1},{1,0},{2,3},{3,2},{4,5},{5,4},{6,7},{7,6},{8,9},{9,8},{10,11... | collective-permute-start | bytes 2359304 | tf_op jit(solution)/shard_map/ppermute | solution.py:698
  242.1 41.8 %collective-permute-start.39 = (bf16[64,6272]{1,0:T(8,128)(2,1)}, bf16[64,6272]{1,0:T(8,128)(2,1)S(1)}, u32[]{:S(2)}, u32[]{:S(2)}) collective-permute-start(bf16[64,6272]{1,0:T(8,128)(2,1)} %add_convert_fusion.2), channel_id=1, source_target_pairs={{0,4},{2,6},{4,8},{6,10},{8,12},{10,14},{12,0},{14,2},{1,5},{3,7},... | collective-permute-start | bytes 2408456 | tf_op jit(solution)/shard_map/ppermute | solution.py:694
  279.6 33.1 %collective-permute-start.32 = (bf16[3060,128]{1,0:T(8,128)(2,1)S(1)}, bf16[3060,128]{1,0:T(8,128)(2,1)S(1)}, u32[]{:S(2)}, u32[]{:S(2)}) collective-permute-start(bf16[3060,128]{1,0:T(8,128)(2,1)S(1)} %get-tuple-element.72), channel_id=1, source_target_pairs={{0,16},{16,0},{1,17},{17,1},{2,18},{18,2},{3,19},{19,3},{4,20},{20... | collective-permute-start | bytes 2350088 | tf_op jit(solution)/shard_map/ppermute | solution.py:698
  281.0 42.6 %collective-permute-start.37 = (bf16[64,6272]{1,0:T(8,128)(2,1)}, bf16[64,6272]{1,0:T(8,128)(2,1)S(1)}, u32[]{:S(2)}, u32[]{:S(2)}) collective-permute-start(bf16[64,6272]{1,0:T(8,128)(2,1)} %get-tuple-element.80), channel_id=1, source_target_pairs={{0,2},{2,0},{4,6},{6,4},{8,10},{10,8},{12,14},{14,12},{1,3},{3,1},... | collective-permute-start | bytes 2408456 | tf_op jit(solution)/shard_map/ppermute | solution.py:690
  282.7 26.3 %collective-permute-start.43 = (bf16[256,768]{1,0:T(8,128)(2,1)S(1)}, bf16[256,768]{1,0:T(8,128)(2,1)S(1)}, u32[]{:S(2)}, u32[]{:S(2)}) collective-permute-start(bf16[256,768]{1,0:T(8,128)(2,1)S(1)} %slice.365), channel_id=1, source_target_pairs={{0,2},{2,0},{4,6},{6,4},{8,10},{10,8},{12,14},{14,12},{1,3},{3,1},... | collective-permute-start | bytes 1179656 | tf_op jit(solution)/shard_map/ppermute | solution.py:690
  286.2 37.3 %collective-permute-start.40 = (bf16[64,6272]{1,0:T(8,128)(2,1)}, bf16[64,6272]{1,0:T(8,128)(2,1)}, u32[]{:S(2)}, u32[]{:S(2)}) collective-permute-start(bf16[64,6272]{1,0:T(8,128)(2,1)} %add_convert_fusion.1), channel_id=1, source_target_pairs={{0,4},{2,6},{4,8},{6,10},{8,12},{10,14},{12,0},{14,2},{1,5},{3,7},... | collective-permute-start | bytes 2408456 | tf_op jit(solution)/shard_map/ppermute | solution.py:694
  309.2 6.9 %collective-permute-start.46 = (bf16[64,768]{1,0:T(8,128)(2,1)S(1)}, bf16[64,768]{1,0:T(8,128)(2,1)S(1)}, u32[]{:S(2)}, u32[]{:S(2)}) collective-permute-start(bf16[64,768]{1,0:T(8,128)(2,1)S(1)} %get-tuple-element.183), channel_id=1, source_target_pairs={{0,4},{2,6},{4,8},{6,10},{8,12},{10,14},{12,0},{14,2},{1,5},{3,7},... | collective-permute-start | bytes 294920 | tf_op jit(solution)/shard_map/ppermute | solution.py:694
  310.0 9.9 %collective-permute-start.45 = (bf16[64,768]{1,0:T(8,128)(2,1)S(1)}, bf16[64,768]{1,0:T(8,128)(2,1)S(1)}, u32[]{:S(2)}, u32[]{:S(2)}) collective-permute-start(bf16[64,768]{1,0:T(8,128)(2,1)S(1)} %get-tuple-element.184), channel_id=1, source_target_pairs={{0,8},{2,10},{4,12},{6,14},{8,0},{10,2},{12,4},{14,6},{1,9},{3,11}... | collective-permute-start | bytes 294920 | tf_op jit(solution)/shard_map/ppermute | solution.py:694
  312.7 7.2 %collective-permute-start.44 = (bf16[64,768]{1,0:T(8,128)(2,1)S(1)}, bf16[64,768]{1,0:T(8,128)(2,1)S(1)}, u32[]{:S(2)}, u32[]{:S(2)}) collective-permute-start(bf16[64,768]{1,0:T(8,128)(2,1)S(1)} %get-tuple-element.182), channel_id=1, source_target_pairs={{0,12},{2,14},{4,0},{6,2},{8,4},{10,6},{12,8},{14,10},{1,13},{3,15... | collective-permute-start | bytes 294920 | tf_op jit(solution)/shard_map/ppermute | solution.py:694
  (31 other events, 333.4 us)
